TPU v7x, 32 devices: a whole 2x2x4 slice. The times are simulated.
32 devices in a mesh: ens: 2 (over x), gx: 8 (over z, y), gy: 2 (over core).
Axes of the slice: x: 2, y: 2, z: 4, core: 2. Of those that a mesh axis runs over, the one named last changes fastest.
Arguments:
- atm_fields: float32 [8, 60, 256, 256], P('ens', None, 'gx', 'gy'), parts along dimension 0, may hold values from -5 to 5
- ocean_fields: float32 [8, 40, 512, 512], P('ens', None, 'gx', 'gy'), parts along dimension 0, may hold values from -5 to 5
- land_sea: int32 [1024, 512], P(('ens', 'gx'), 'gy'), parts along dimension 0, may hold values 0 or 1
- sea_weights: float32 [768, 128, 128], P(('ens', 'gx', 'gy')), parts along dimension 0, may hold values from -0.5 to 0.5
- sea_dest: int32 [768, 1], P(('ens', 'gx', 'gy')), parts along dimension 0, may hold values from 0 to 15; in each aligned block of 24 rows (0 to 23, 24 to 47, ...) at most 2 rows name the same one
- sea_source: int32 [768], P(('ens', 'gx', 'gy')), parts along dimension 0, may hold values from 0 to 127
- sea_window: int32 [768], P(('ens', 'gx', 'gy')), parts along dimension 0, may hold values from 0 to 31
- air_weights: float32 [768, 128, 128], P(('ens', 'gx', 'gy')), parts along dimension 0, may hold values from -0.5 to 0.5
- air_dest: int32 [768, 1], P(('ens', 'gx', 'gy')), parts along dimension 0, may hold values from 0 to 15; in each aligned block of 24 rows (0 to 23, 24 to 47, ...) at most 2 rows name the same one
- air_source: int32 [768], P(('ens', 'gx', 'gy')), parts along dimension 0, may hold values from 0 to 31
- air_window: int32 [768], P(('ens', 'gx', 'gy')), parts along dimension 0, may hold values from 0 to 127
Outputs:
- air_next: float32 [4, 60, 256, 256], P('ens', None, 'gx', 'gy'), parts along dimension 0
- sea_next: float32 [4, 40, 512, 512], P('ens', None, 'gx', 'gy'), parts along dimension 0
There are 2 independent parts, one for each index of `ens`. A program takes and returns all parts, laid end to end along the dimension named above; each array names one. Nothing has to cross between parts.
Inputs may be any that keep to these rules, and one draw needn't show every extreme that they name: `sea_dest`: in each aligned block of 24 rows (the blocks of one source tile) no tile is named by more than 2 rows; some block names one tile exactly 2 times. `air_dest`: in each aligned block of 24 rows (the blocks of one source tile) no tile is named by more than 2 rows; some block names one tile exactly 2 times.
All inputs are finite; a program needn't handle non-finite values. No bound on the sum of `land_sea` on one device may be relied on, other than what follows from the above.
Results may differ from a plain program's by a relative error of at most 0.000071.
Values sent between devices are 32-bit elements; how exact they have to be, the bound alone decides.
No kernel may reach another device: no remote copies, remote signals or barrier semaphores. Data moves between devices by JAX's collectives and lax.ppermute only.
A program may use at most 192 MiB of HBM per device.

v0:
```python
import functools

import jax
import jax.numpy as jnp
from jax import lax
from jax.experimental import pallas as pl
from jax.experimental.pallas import tpu as pltpu
from jax.sharding import PartitionSpec as P

WIN = 128
CAP = 2
ROWS = 4
LANES = 128
SUB = 8

time_step = 0.1
diffusion = 0.2
VMEM_LIMIT = 56 * 1024 * 1024


def lane_of(shape):
    return lax.broadcasted_iota(jnp.int32, shape, len(shape) - 1)


def row_of(shape):
    return lax.broadcasted_iota(jnp.int32, shape, len(shape) - 2)


def send_blocks(pick, count, weights_ref, dest_ref, window_ref, picked_ref, counts_ref, out_ref):
    blocks = weights_ref.shape[0]
    out_ref[...] = jnp.zeros_like(out_ref)

    def clear(d, carry):
        counts_ref[d] = 0
        return carry

    lax.fori_loop(0, out_ref.shape[0], clear, 0)
    picked_ref[...] = jnp.zeros_like(picked_ref)
    for k in range(blocks):
        for f in range(count):
            picked_ref[k, pl.ds(f, 1), :] = pick(k, f)
    row = row_of((SUB, LANES))
    lane = lane_of((SUB, LANES))
    for k in range(blocks):
        values = picked_ref[k]
        high = values.astype(jnp.bfloat16)
        low = (values - high.astype(jnp.float32)).astype(jnp.bfloat16)
        left = jnp.concatenate([high.astype(jnp.float32), low.astype(jnp.float32)], axis=0).astype(jnp.bfloat16)
        weight = weights_ref[k]
        weight_high = weight.astype(jnp.bfloat16)
        weight_low = (weight - weight_high.astype(jnp.float32)).astype(jnp.bfloat16)
        right = jnp.concatenate([weight_high, weight_low], axis=0)
        product = lax.dot_general(left, right, (((1,), (1,)), ((), ())), preferred_element_type=jnp.float32)
        total = product[:SUB, :WIN] + (product[SUB:, :WIN] + product[:SUB, WIN:])
        d = dest_ref[k, 0]
        slot = counts_ref[d]
        counts_ref[d] = slot + 1
        onehot = jnp.where(lane == window_ref[k], 1.0, 0.0)
        total = jnp.where(row == ROWS - 1, onehot, jnp.where(row < count, total, 0.0))
        total = jnp.where(slot == 0, total, jnp.concatenate([total[ROWS:], total[:ROWS]], axis=0))
        out_ref[d] = out_ref[d] + total


def receive_blocks(arrived_ref, count):
    slots = arrived_ref.shape[0] // ROWS
    onehot = arrived_ref[pl.ds(ROWS - 1, slots, stride=ROWS), :]
    fields = [arrived_ref[pl.ds(f, slots, stride=ROWS), :] for f in range(count)]
    return [
        lax.dot_general(
            onehot, field, (((0,), (0,)), ((), ())), precision=lax.Precision.HIGHEST, preferred_element_type=jnp.float32
        )
        for field in fields
    ]


def sea_send_kernel(
    dest_ref, source_ref, window_ref, ocean_ref, weights_ref, out_ref, picked_ref, counts_ref, surface_ref
):
    rows, cols = ocean_ref.shape[2:]
    halves = cols // WIN
    for f in range(3):
        for h in range(halves):
            surface_ref[f, pl.ds(h, rows, stride=halves), :] = ocean_ref[(0, 2, 3)[f], 0, :, pl.ds(h * WIN, WIN)]

    def pick(k, f):
        return surface_ref[f, pl.ds(source_ref[k], 1), :]

    send_blocks(pick, 3, weights_ref, dest_ref, window_ref, picked_ref, counts_ref, out_ref)


def sea_send(tiles, ocean, weights, dest, source, window):
    blocks = weights.shape[0]
    smem = pl.BlockSpec(memory_space=pltpu.SMEM)
    return pl.pallas_call(
        sea_send_kernel,
        grid=(1,),
        out_shape=jax.ShapeDtypeStruct((tiles, CAP * ROWS, WIN), jnp.float32),
        in_specs=[
            smem,
            smem,
            smem,
            pl.BlockSpec((4, 1) + ocean.shape[2:], lambda i: (0, 0, 0, 0)),
            pl.BlockSpec(weights.shape, lambda i: (0, 0, 0)),
        ],
        out_specs=pl.BlockSpec((tiles, CAP * ROWS, WIN), lambda i: (0, 0, 0)),
        scratch_shapes=[
            pltpu.VMEM((blocks, SUB, WIN), jnp.float32),
            pltpu.SMEM((tiles,), jnp.int32),
            pltpu.VMEM((3, ocean.shape[2] * ocean.shape[3] // WIN, WIN), jnp.float32),
        ],
        compiler_params=pltpu.CompilerParams(vmem_limit_bytes=VMEM_LIMIT),
        cost_estimate=pl.CostEstimate(flops=blocks * 2 * 16 * 128 * 256, bytes_accessed=2000000, transcendentals=0),
        name="sea_send",
    )(dest, source, window, ocean, weights)


def air_send_kernel(
    dest_ref, source_ref, window_ref, arrived_ref, atm_ref, weights_ref, out_ref, flux_ref, picked_ref, counts_ref
):
    rows = atm_ref.shape[2]
    on_air = [field[:rows] for field in receive_blocks(arrived_ref, 3)]
    relative_u = atm_ref[2, 0] - on_air[1]
    relative_v = atm_ref[3, 0] - on_air[2]
    wind_speed = jnp.sqrt(relative_u * relative_u + relative_v * relative_v + 1.0)
    flux_ref[0] = 0.5 * wind_speed * (on_air[0] - atm_ref[0, 0])
    flux_ref[1] = 0.4 * wind_speed * (0.8 * on_air[0] - atm_ref[1, 0])

    def pick(k, f):
        return flux_ref[f, pl.ds(source_ref[k], 1), :]

    send_blocks(pick, 2, weights_ref, dest_ref, window_ref, picked_ref, counts_ref, out_ref)


def air_send(arrived, atm, weights, dest, source, window):
    blocks = weights.shape[0]
    tiles = arrived.shape[0]
    rows, cols = atm.shape[2:]
    smem = pl.BlockSpec(memory_space=pltpu.SMEM)
    return pl.pallas_call(
        air_send_kernel,
        grid=(1,),
        out_shape=(
            jax.ShapeDtypeStruct((tiles, CAP * ROWS, WIN), jnp.float32),
            jax.ShapeDtypeStruct((2, rows, cols), jnp.float32),
        ),
        in_specs=[
            smem,
            smem,
            smem,
            pl.BlockSpec((tiles * CAP * ROWS, WIN), lambda i: (0, 0)),
            pl.BlockSpec((4, 1, rows, cols), lambda i: (0, 0, 0, 0)),
            pl.BlockSpec(weights.shape, lambda i: (0, 0, 0)),
        ],
        out_specs=(
            pl.BlockSpec((tiles, CAP * ROWS, WIN), lambda i: (0, 0, 0)),
            pl.BlockSpec((2, rows, cols), lambda i: (0, 0, 0)),
        ),
        scratch_shapes=[pltpu.VMEM((blocks, SUB, WIN), jnp.float32), pltpu.SMEM((tiles,), jnp.int32)],
        compiler_params=pltpu.CompilerParams(vmem_limit_bytes=VMEM_LIMIT),
        cost_estimate=pl.CostEstimate(flops=blocks * 2 * 16 * 128 * 256, bytes_accessed=2000000, transcendentals=0),
        name="air_send",
    )(dest, source, window, arrived.reshape(tiles * CAP * ROWS, WIN), atm, weights)


def sea_forcing_kernel(arrived_ref, land_ref, before_ref, after_ref, summed_ref):
    rows, cols = land_ref.shape
    halves = cols // WIN
    for f, field in enumerate(receive_blocks(arrived_ref, 2)):
        summed_ref[f] = field
        for h in range(halves):
            span = pl.ds(h * WIN, WIN)
            forcing = summed_ref[f, pl.ds(h, rows, stride=halves), :] * (-0.5, 0.3)[f]
            change = jnp.where(land_ref[:, span] == 1, time_step * forcing, 0.0)
            after_ref[f, 0, :, span] = before_ref[f, 0, :, span] + change


def add_sea_forcing(arrived, land, sea_next):
    tiles = arrived.shape[0]
    rows, cols = land.shape
    return pl.pallas_call(
        sea_forcing_kernel,
        grid=(1,),
        out_shape=jax.ShapeDtypeStruct(sea_next.shape, jnp.float32),
        in_specs=[
            pl.BlockSpec((tiles * CAP * ROWS, WIN), lambda i: (0, 0)),
            pl.BlockSpec((rows, cols), lambda i: (0, 0)),
            pl.BlockSpec((2, 1, rows, cols), lambda i: (0, 0, 0, 0)),
        ],
        out_specs=pl.BlockSpec((2, 1, rows, cols), lambda i: (0, 0, 0, 0)),
        scratch_shapes=[pltpu.VMEM((2, rows * cols // WIN, WIN), jnp.float32)],
        input_output_aliases={2: 0},
        compiler_params=pltpu.CompilerParams(vmem_limit_bytes=VMEM_LIMIT),
        cost_estimate=pl.CostEstimate(flops=4000000, bytes_accessed=600000, transcendentals=0),
        name="sea_forcing",
    )(arrived.reshape(tiles * CAP * ROWS, WIN), land, sea_next)


STEPS = 5


def padded_levels(levels):
    return -(-levels // SUB) * SUB


def edges_kernel(gy_ref, atm_ref, half_q_ref, half_v_ref, low_ref, high_ref, xlow_ref, xhigh_ref, y_ref):
    step = pl.program_id(0)
    air_levels, air_rows = atm_ref.shape[1:3]
    sea_levels, sea_rows = half_q_ref.shape[1:3]
    all_air, all_sea = air_levels * STEPS, sea_levels * STEPS
    halves = low_ref.shape[3] // WIN
    pitch = padded_levels(all_air)

    @pl.when(step == 0)
    def _():
        xlow_ref[...] = jnp.zeros_like(xlow_ref)
        xhigh_ref[...] = jnp.zeros_like(xhigh_ref)
        y_ref[...] = jnp.zeros_like(y_ref)

    for f in range(3):
        for level in range(air_levels):
            to = pl.ds(f * pitch + step * air_levels + level, 1)
            xlow_ref[to, :] = atm_ref[f, level, pl.ds(0, 1), :]
            xhigh_ref[to, :] = atm_ref[f, level, pl.ds(air_rows - 1, 1), :]
        for h in range(halves):
            for level in range(sea_levels):
                to = pl.ds(3 * pitch + (f * halves + h) * all_sea + step * sea_levels + level, 1)
                span = pl.ds(h * WIN, WIN)
                xlow_ref[to, :] = low_ref[f, level, pl.ds(0, 1), span]
                xhigh_ref[to, :] = high_ref[f, level, pl.ds(SUB - 1, 1), span]

    edge = jnp.where(gy_ref[0] == 0, LANES - 1, 0)

    def put(total, column, to, lane):
        return jnp.where(lane == to, pltpu.roll(column, (to - edge + LANES) % LANES, 1), total)

    lane = lane_of((air_rows, LANES))
    tracers, v = y_ref[:air_rows], y_ref[air_rows : 2 * air_rows]
    for level in range(air_levels):
        to = step * air_levels + level
        tracers = put(tracers, atm_ref[0, level], to, lane)
        tracers = put(tracers, atm_ref[1, level], LANES // 2 + to, lane)
        v = put(v, atm_ref[3, level], to, lane)
    y_ref[:air_rows] = tracers
    y_ref[air_rows : 2 * air_rows] = v
    lane = lane_of((sea_rows, LANES))
    total = y_ref[2 * air_rows :]
    for level in range(sea_levels):
        to = step * sea_levels + level
        total = put(total, half_q_ref[0, level], to, lane)
        total = put(total, half_q_ref[1, level], all_sea + to, lane)
        total = put(total, half_v_ref[0, level], 2 * all_sea + to, lane)
    y_ref[2 * air_rows :] = total


def edges(gy, atm, ocean):
    air_levels, air_rows, _ = atm.shape[1:]
    sea_levels, sea_rows, sea_cols = ocean.shape[1:]
    a, o = air_levels // STEPS, sea_levels // STEPS
    xrows = 3 * padded_levels(air_levels) + 3 * sea_levels * (sea_cols // WIN)
    yrows = 2 * air_rows + sea_rows
    last = sea_cols // WIN - 1
    x_shape = jax.ShapeDtypeStruct((xrows, LANES), jnp.float32)
    return pl.pallas_call(
        edges_kernel,
        grid_spec=pltpu.PrefetchScalarGridSpec(
            num_scalar_prefetch=1,
            grid=(STEPS,),
            in_specs=[
                pl.BlockSpec((4, a, air_rows, LANES), lambda i, gy: (0, i, 0, 0)),
                pl.BlockSpec((2, o, sea_rows, LANES), lambda i, gy: (0, i, 0, last * (1 - gy[0]))),
                pl.BlockSpec((1, o, sea_rows, LANES), lambda i, gy: (3, i, 0, last * (1 - gy[0]))),
                pl.BlockSpec((3, o, SUB, sea_cols), lambda i, gy: (0, i, 0, 0)),
                pl.BlockSpec((3, o, SUB, sea_cols), lambda i, gy: (0, i, sea_rows // SUB - 1, 0)),
            ],
            out_specs=[
                pl.BlockSpec((xrows, LANES), lambda i, gy: (0, 0)),
                pl.BlockSpec((xrows, LANES), lambda i, gy: (0, 0)),
                pl.BlockSpec((yrows, LANES), lambda i, gy: (0, 0)),
            ],
        ),
        out_shape=(x_shape, x_shape, jax.ShapeDtypeStruct((yrows, LANES), jnp.float32)),
        compiler_params=pltpu.CompilerParams(vmem_limit_bytes=VMEM_LIMIT),
        cost_estimate=pl.CostEstimate(flops=2000000, bytes_accessed=10000000, transcendentals=0),
        name="edges",
    )(gy, atm, ocean, ocean, ocean, ocean)


def step_level(fields, west, east, south, write):
    row = row_of((SUB, LANES))
    lane = lane_of((SUB, LANES))
    groups, halves = fields.groups, fields.halves
    first_row, last_row = row == 0, row == SUB - 1
    first_lane, last_lane = lane == 0, lane == LANES - 1

    def along_x(f, h, scale):
        tiles = [fields(f, r, h) for r in range(groups)]
        if scale is not None:
            tiles = [scale * t for t in tiles]
        down = [pltpu.roll(t, 1, 0) for t in tiles]
        up = [pltpu.roll(t, SUB - 1, 0) for t in tiles]
        before = [jnp.broadcast_to(west(f, h), (SUB, LANES))] + down[:-1]
        after = up[1:] + [jnp.broadcast_to(east(f, h), (SUB, LANES))]
        if scale is not None:
            before[0], after[-1] = scale * before[0], scale * after[-1]
        lows = [jnp.where(first_row, b, d) for b, d in zip(before, down)]
        highs = [jnp.where(last_row, a, u) for a, u in zip(after, up)]
        return tiles, lows, highs

    def along_y(f, r, tiles, scale):
        beyond = south(f, r)
        if scale is not None:
            beyond = scale * beyond
        right = [pltpu.roll(t, 1, 1) for t in tiles]
        left = [pltpu.roll(t, LANES - 1, 1) for t in tiles]
        lows = [jnp.where(first_lane, b, t) for b, t in zip([beyond] + right[:-1], right)]
        highs = [jnp.where(last_lane, b, t) for b, t in zip(left[1:] + [beyond], left)]
        return lows, highs

    scale = 0.25 * time_step
    mixing = time_step * diffusion
    moved = [[along_x(f, h, scale if f == 2 else None) for h in range(halves)] for f in range(3)]
    for r in range(groups):
        v = [scale * fields(3, r, h) for h in range(halves)]
        v_low, v_high = along_y(3, r, v, scale)
        sides = [along_y(f, r, [moved[f][h][0][r] for h in range(halves)], None) for f in range(2)]
        for h in range(halves):
            u, u_low, u_high = (part[r] for part in moved[2][h])
            centre = (1.0 - 4.0 * mixing) + ((u_low - u_high) + (v_low[h] - v_high[h]))
            x_high, x_low = (mixing - u) - u_high, (mixing + u) + u_low
            y_high, y_low = (mixing - v[h]) - v_high[h], (mixing + v[h]) + v_low[h]
            for f in range(2):
                q, q_low, q_high = (part[r] for part in moved[f][h])
                new = centre * q + (x_high * q_high + x_low * q_low)
                new = new + (y_high * sides[f][1][h] + y_low * sides[f][0][h])
                write(f, r, h, new, q)


class Fields:
    def __init__(self, ref, level):
        self.ref, self.level = ref, level
        self.groups, self.halves = ref.shape[2] // SUB, ref.shape[3] // LANES

    def __call__(self, f, r, h):
        return self.ref[f, self.level, pl.ds(r * SUB, SUB), pl.ds(h * LANES, LANES)]


def transport_kernel(gy_ref, atm_ref, ocean_ref, land_ref, flux_ref, xlow_ref, xhigh_ref, y_ref, air_ref, sea_ref):
    step = pl.program_id(0)
    steps = pl.num_programs(0)
    air_levels, air_rows = atm_ref.shape[1:3]
    sea_levels, sea_rows, sea_cols = ocean_ref.shape[1:]
    all_air, all_sea = STEPS_T * air_levels, STEPS_T * sea_levels
    halves = sea_cols // LANES
    pitch = padded_levels(all_air)
    edge = jnp.where(gy_ref[0] == 0, LANES - 1, 0)
    at_edge = lane_of((SUB, LANES)) == edge

    def column(start, r, at):
        tile = y_ref[pl.ds(start + r * SUB, SUB), :]
        return jnp.where(at_edge, pltpu.roll(tile, (edge - at + LANES) % LANES, 1), 0.0)

    def air_level(level, carry):
        here = step * air_levels + level

        def beyond(f, r):
            start = air_rows if f == 3 else 0
            return column(start, r, (LANES // 2 if f == 1 else 0) + here)

        def write(f, r, h, new, q):
            air_ref[f, level, pl.ds(r * SUB, SUB), :] = new

        step_level(
            Fields(atm_ref, level),
            lambda f, h: xlow_ref[pl.ds(f * pitch + here, 1), :],
            lambda f, h: xhigh_ref[pl.ds(f * pitch + here, 1), :],
            beyond,
            write,
        )
        return carry

    lax.fori_loop(0, air_levels, air_level, 0)

    @pl.when(step == 0)
    def _():
        for f in range(2):
            air_ref[f, 0] = air_ref[f, 0] + time_step * flux_ref[f]

    def sea_level(level, carry):
        here = step * sea_levels + level

        def beyond(f, r):
            return column(2 * air_rows, r, (2 if f == 3 else f) * all_sea + here)

        def write(f, r, h, new, q):
            rows, span = pl.ds(r * SUB, SUB), pl.ds(h * LANES, LANES)
            sea_ref[f, level, rows, span] = jnp.where(land_ref[rows, span] == 1, new, q)

        step_level(
            Fields(ocean_ref, level),
            lambda f, h: xlow_ref[pl.ds(3 * pitch + (f * halves + h) * all_sea + here, 1), :],
            lambda f, h: xhigh_ref[pl.ds(3 * pitch + (f * halves + h) * all_sea + here, 1), :],
            beyond,
            write,
        )
        return carry

    lax.fori_loop(0, sea_levels, sea_level, 0)


STEPS_T = 10


def transport(gy, atm, ocean, land, flux, xlow, xhigh, y):
    air_levels, air_rows, _ = atm.shape[1:]
    sea_levels, sea_rows, sea_cols = ocean.shape[1:]
    a, o = air_levels // STEPS_T, sea_levels // STEPS_T

    def whole(array):
        return pl.BlockSpec(array.shape, lambda i, gy: (0,) * array.ndim)

    return pl.pallas_call(
        transport_kernel,
        grid_spec=pltpu.PrefetchScalarGridSpec(
            num_scalar_prefetch=1,
            grid=(STEPS_T,),
            in_specs=[
                pl.BlockSpec((4, a, air_rows, LANES), lambda i, gy: (0, i, 0, 0)),
                pl.BlockSpec((4, o, sea_rows, sea_cols), lambda i, gy: (0, i, 0, 0)),
                whole(land),
                whole(flux),
                whole(xlow),
                whole(xhigh),
                whole(y),
            ],
            out_specs=[
                pl.BlockSpec((2, a, air_rows, LANES), lambda i, gy: (0, i, 0, 0)),
                pl.BlockSpec((2, o, sea_rows, sea_cols), lambda i, gy: (0, i, 0, 0)),
            ],
        ),
        out_shape=(
            jax.ShapeDtypeStruct((2,) + atm.shape[1:], jnp.float32),
            jax.ShapeDtypeStruct((2,) + ocean.shape[1:], jnp.float32),
        ),
        compiler_params=pltpu.CompilerParams(vmem_limit_bytes=VMEM_LIMIT),
        cost_estimate=pl.CostEstimate(flops=60000000, bytes_accessed=22000000, transcendentals=0),
        name="transport",
    )(gy, atm, ocean, land, flux, xlow, xhigh, y)


def body(
    atm_fields,
    ocean_fields,
    land_sea,
    sea_weights,
    sea_dest,
    sea_source,
    sea_window,
    air_weights,
    air_dest,
    air_source,
    air_window,
):
    width_x, width_y = lax.axis_size("gx"), lax.axis_size("gy")
    assert width_y == 2
    tiles = width_x * width_y
    gy = lax.axis_index("gy").astype(jnp.int32).reshape(1)
    exchange = functools.partial(lax.all_to_all, axis_name=("gx", "gy"), split_axis=0, concat_axis=0, tiled=True)
    forward = [(i, i + 1) for i in range(width_x - 1)]
    backward = [(i + 1, i) for i in range(width_x - 1)]

    to_air = sea_send(tiles, ocean_fields, sea_weights, sea_dest, sea_source, sea_window)
    on_air = exchange(to_air)
    low, high, side = edges(gy, atm_fields, ocean_fields)
    side = lax.ppermute(side, "gy", [(0, 1), (1, 0)])
    xlow = lax.ppermute(high, "gx", forward)
    xhigh = lax.ppermute(low, "gx", backward)
    to_sea, fluxes = air_send(on_air, atm_fields, air_weights, air_dest, air_source, air_window)
    on_sea = exchange(to_sea)
    air_next, sea_next = transport(gy, atm_fields, ocean_fields, land_sea, fluxes, xlow, xhigh, side)
    sea_next = add_sea_forcing(on_sea, land_sea, sea_next)
    return (air_next, sea_next)


def solution(mesh):
    placed = (
        P("ens", None, "gx", "gy"),
        P("ens", None, "gx", "gy"),
        P(("ens", "gx"), "gy"),
        P(("ens", "gx", "gy"), None, None),
        P(("ens", "gx", "gy"), None),
        P(("ens", "gx", "gy")),
        P(("ens", "gx", "gy")),
        P(("ens", "gx", "gy"), None, None),
        P(("ens", "gx", "gy"), None),
        P(("ens", "gx", "gy")),
        P(("ens", "gx", "gy")),
    )
    return jax.shard_map(
        body,
        mesh=mesh,
        in_specs=placed,
        out_specs=(P("ens", None, "gx", "gy"), P("ens", None, "gx", "gy")),
        check_vma=False,
    )
```

profile of v0, /device:TPU:0, one launch (start us, length us, event | category | flops | bytes accessed | tf_op | source)
XLA Modules:
  0.0 57.9 jit_solution(5990362131781790598)
XLA Ops:
  0.6 1.3 %copy.14.dest_ref = s32[24,1]{1,0:T(8,128)} copy(s32[24,1]{0,1:T(1,128)} %param.15) | data formatting | bytes 192 | tf_op args[4]
  2.0 2.8 %sea_send.1 = f32[16,8,128]{2,1,0:T(8,128)} custom-call(s32[24,1]{1,0:T(8,128)} %copy.14.dest_ref, s32[24]{0:T(128)} %source_ref.2, s32[24]{0:T(128)} %window_ref.2, f32[4,40,64,256]{3,2,1,0:T(8,128)} %ocean_ref.3, f32[24,128,128]{2,1,0:T(8,128)} %weights_ref.2), custom_call_target="tpu_custom_call" | custom-call | flops 25165824 | bytes 2000000 | tf_op jit(solution)/shard_map/sea_send/pallas_call | solution.py:94
  4.7 7.4 %all-to-all-start = ((f32[16,8,128]{2,1,0:T(8,128)}), f32[16,8,128]{2,1,0:T(8,128)S(1)}, u32[]{:S(2)}, u32[]{:S(2)}) async-start(f32[16,8,128]{2,1,0:T(8,128)} %sea_send.1), calls=%async_computation | async-start | bytes 131072 | tf_op jit(solution)/shard_map/all_to_all | solution.py:472
  12.1 0.0 copy-start.5
  12.2 6.7 %edges.1 = (f32[432,128]{1,0:T(8,128)}, f32[432,128]{1,0:T(8,128)}, f32[128,128]{1,0:T(8,128)}) custom-call(s32[1]{0:T(128)} %bitcast.gy_ref, f32[4,60,32,128]{3,2,1,0:T(8,128)} %atm_ref.5, f32[4,40,64,256]{3,2,1,0:T(8,128)} %ocean_ref.3, f32[4,40,64,256]{3,2,1,0:T(8,128)} %ocean_ref.3, f32[4,40,64,256]{3,2,1,0:T(8,128)} %ocean_ref.3, ...), custom_call_target="tpu_custom_call" | custom-call | flops 2000000 | bytes 10000000 | tf_op jit(solution)/shard_map/edges/pallas_call | solution.py:263
  18.8 0.0 copy-start.6
  18.8 4.0 %collective-permute-start = (f32[432,128]{1,0:T(8,128)}, f32[432,128]{1,0:T(8,128)S(1)}, u32[]{:S(2)}, u32[]{:S(2)}) collective-permute-start(f32[432,128]{1,0:T(8,128)} %get-tuple-element.10), channel_id=1, source_target_pairs={{0,2},{2,4},{4,6},{6,8},{8,10},{10,12},{12,14},{1,3},{3,5},{5,7},{... | collective-permute-start | bytes 663560 | tf_op jit(solution)/shard_map/ppermute | solution.py:475
  22.8 1.3 %collective-permute-start.1 = (f32[432,128]{1,0:T(8,128)}, f32[432,128]{1,0:T(8,128)S(1)}, u32[]{:S(2)}, u32[]{:S(2)}) collective-permute-start(f32[432,128]{1,0:T(8,128)} %get-tuple-element.11), channel_id=1, source_target_pairs={{2,0},{4,2},{6,4},{8,6},{10,8},{12,10},{14,12},{3,1},{5,3},{7,5},{... | collective-permute-start | bytes 663560 | tf_op jit(solution)/shard_map/ppermute | solution.py:476
  24.1 0.0 copy-done.5
  24.1 0.7 %copy.15.dest_ref = s32[24,1]{1,0:T(8,128)} copy(s32[24,1]{0,1:T(1,128)S(1)} %copy-done.5) | data formatting | bytes 192 | tf_op args[8]
  24.8 0.0 all-to-all-done
  24.8 0.0 copy-start
  24.8 0.6 %copy-done = f32[16,8,128]{2,1,0:T(8,128)} copy-done((f32[16,8,128]{2,1,0:T(8,128)}, f32[16,8,128]{2,1,0:T(8,128)S(1)}, u32[]{:S(2)}) %copy-start) | copy-done | bytes 65560
  25.4 3.2 %air_send.1 = (f32[16,8,128]{2,1,0:T(8,128)}, f32[2,32,128]{2,1,0:T(8,128)}) custom-call(s32[24,1]{1,0:T(8,128)} %copy.15.dest_ref, s32[24]{0:T(128)} %source_ref.3, s32[24]{0:T(128)} %window_ref.3, f32[128,128]{1,0:T(8,128)} %bitcast.3, f32[4,60,32,128]{3,2,1,0:T(8,128)} %atm_ref.5, f32[24,128,128]{2,1,0:T(8,128)} %weights_ref.3), custom_call_target="tpu_custom_call" | custom-call | flops 25165824 | bytes 2000000 | tf_op jit(solution)/shard_map/air_send/pallas_call | solution.py:139
  28.6 6.7 %all-to-all-start.1 = ((f32[16,8,128]{2,1,0:T(8,128)}), f32[16,8,128]{2,1,0:T(8,128)S(1)}, u32[]{:S(2)}, u32[]{:S(2)}) async-start(f32[16,8,128]{2,1,0:T(8,128)} %get-tuple-element.14), calls=%async_computation.1 | async-start | bytes 131072 | tf_op jit(solution)/shard_map/all_to_all | solution.py:478
  35.3 0.0 copy-done.6
  35.3 0.5 collective-permute-start.2
  35.8 0.9 %collective-permute-done.2.y_ref = f32[128,128]{1,0:T(8,128)S(1)} collective-permute-done((f32[128,128]{1,0:T(8,128)S(1)}, f32[128,128]{1,0:T(8,128)S(1)}, u32[]{:S(2)}, u32[]{:S(2)}) %collective-permute-start.2) | collective-permute-done | bytes 65568 | tf_op jit(solution)/shard_map/ppermute | solution.py:474
  36.7 0.0 copy-start.4
  36.7 0.0 collective-permute-done.xlow_ref
  36.7 0.0 copy-start.2
  36.7 0.0 collective-permute-done.1.xhigh_ref
  36.7 0.0 copy-start.3
  36.7 0.6 %copy-done.4 = f32[128,128]{1,0:T(8,128)} copy-done((f32[128,128]{1,0:T(8,128)}, f32[128,128]{1,0:T(8,128)S(1)}, u32[]{:S(2)}) %copy-start.4) | copy-done | bytes 65560
  37.3 0.1 copy-done.2
  37.4 0.1 copy-done.3
  37.5 17.8 %transport.1 = (f32[2,60,32,128]{3,2,1,0:T(8,128)}, f32[2,40,64,256]{3,2,1,0:T(8,128)}) custom-call(s32[1]{0:T(128)} %bitcast.gy_ref, f32[4,60,32,128]{3,2,1,0:T(8,128)} %atm_ref.5, f32[4,40,64,256]{3,2,1,0:T(8,128)} %ocean_ref.3, s32[64,256]{1,0:T(8,128)} %land_ref.3, f32[2,32,128]{2,1,0:T(8,128)} %get-tuple-element.9.flux_ref, f32[432,128]{1,0:T(8,128)} %copy-done.2, ...), custom_call_target="tpu_custom_call" | custom-call | flops 60000000 | bytes 22000000 | tf_op jit(solution)/shard_map/transport/pallas_call | solution.py:421
  55.3 0.0 all-to-all-done.1
  55.4 0.0 copy-start.1
  55.4 0.6 %copy-done.1 = f32[16,8,128]{2,1,0:T(8,128)} copy-done((f32[16,8,128]{2,1,0:T(8,128)}, f32[16,8,128]{2,1,0:T(8,128)S(1)}, u32[]{:S(2)}) %copy-start.1) | copy-done | bytes 65560
  56.0 2.0 %sea_forcing.1 = f32[2,40,64,256]{3,2,1,0:T(8,128)} custom-call(f32[128,128]{1,0:T(8,128)} %bitcast.4, s32[64,256]{1,0:T(8,128)} %land_ref.3, f32[2,40,64,256]{3,2,1,0:T(8,128)} %get-tuple-element.15.before_ref), custom_call_target="tpu_custom_call", output_to_operand_aliasing={{}: (2, {})} | custom-call | flops 4000000 | bytes 600000 | tf_op jit(solution)/shard_map/sea_forcing/pallas_call | solution.py:180
Async XLA Ops:
  4.7 20.0 %all-to-all-start = ((f32[16,8,128]{2,1,0:T(8,128)}), f32[16,8,128]{2,1,0:T(8,128)S(1)}, u32[]{:S(2)}, u32[]{:S(2)}) async-start(f32[16,8,128]{2,1,0:T(8,128)} %sea_send.1), calls=%async_computation | async-start | bytes 131072 | tf_op jit(solution)/shard_map/all_to_all | solution.py:472
  12.1 11.9 %copy-start.5 = (s32[24,1]{0,1:T(1,128)S(1)}, s32[24,1]{0,1:T(1,128)}, u32[]{:S(2)}) copy-start(s32[24,1]{0,1:T(1,128)} %param.19) | copy-start | bytes 292
  18.8 16.5 %copy-start.6 = (f32[128,128]{1,0:T(8,128)S(1)}, f32[128,128]{1,0:T(8,128)}, u32[]{:S(2)}) copy-start(f32[128,128]{1,0:T(8,128)} %get-tuple-element.12) | copy-start | bytes 196612
  18.8 17.9 %collective-permute-start = (f32[432,128]{1,0:T(8,128)}, f32[432,128]{1,0:T(8,128)S(1)}, u32[]{:S(2)}, u32[]{:S(2)}) collective-permute-start(f32[432,128]{1,0:T(8,128)} %get-tuple-element.10), channel_id=1, source_target_pairs={{0,2},{2,4},{4,6},{6,8},{8,10},{10,12},{12,14},{1,3},{3,5},{5,7},{... | collective-permute-start | bytes 663560 | tf_op jit(solution)/shard_map/ppermute | solution.py:475
  22.8 13.9 %collective-permute-start.1 = (f32[432,128]{1,0:T(8,128)}, f32[432,128]{1,0:T(8,128)S(1)}, u32[]{:S(2)}, u32[]{:S(2)}) collective-permute-start(f32[432,128]{1,0:T(8,128)} %get-tuple-element.11), channel_id=1, source_target_pairs={{2,0},{4,2},{6,4},{8,6},{10,8},{12,10},{14,12},{3,1},{5,3},{7,5},{... | collective-permute-start | bytes 663560 | tf_op jit(solution)/shard_map/ppermute | solution.py:476
  24.8 0.6 %copy-start = (f32[16,8,128]{2,1,0:T(8,128)}, f32[16,8,128]{2,1,0:T(8,128)S(1)}, u32[]{:S(2)}) copy-start(f32[16,8,128]{2,1,0:T(8,128)S(1)} %all-to-all-done) | copy-start | bytes 196612
  28.6 26.8 %all-to-all-start.1 = ((f32[16,8,128]{2,1,0:T(8,128)}), f32[16,8,128]{2,1,0:T(8,128)S(1)}, u32[]{:S(2)}, u32[]{:S(2)}) async-start(f32[16,8,128]{2,1,0:T(8,128)} %get-tuple-element.14), calls=%async_computation.1 | async-start | bytes 131072 | tf_op jit(solution)/shard_map/all_to_all | solution.py:478
  35.3 1.4 %collective-permute-start.2 = (f32[128,128]{1,0:T(8,128)S(1)}, f32[128,128]{1,0:T(8,128)S(1)}, u32[]{:S(2)}, u32[]{:S(2)}) collective-permute-start(f32[128,128]{1,0:T(8,128)S(1)} %copy-done.6), channel_id=1, source_target_pairs={{0,1},{1,0},{2,3},{3,2},{4,5},{5,4},{6,7},{7,6},{8,9},{9,8},{10,11... | collective-permute-start | bytes 196616 | tf_op jit(solution)/shard_map/ppermute | solution.py:474
  36.7 0.6 %copy-start.4 = (f32[128,128]{1,0:T(8,128)}, f32[128,128]{1,0:T(8,128)S(1)}, u32[]{:S(2)}) copy-start(f32[128,128]{1,0:T(8,128)S(1)} %collective-permute-done.2.y_ref) | copy-start | bytes 196612
  36.7 0.7 %copy-start.2 = (f32[432,128]{1,0:T(8,128)}, f32[432,128]{1,0:T(8,128)S(1)}, u32[]{:S(2)}) copy-start(f32[432,128]{1,0:T(8,128)S(1)} %collective-permute-done.xlow_ref) | copy-start | bytes 663556
  36.7 0.8 %copy-start.3 = (f32[432,128]{1,0:T(8,128)}, f32[432,128]{1,0:T(8,128)S(1)}, u32[]{:S(2)}) copy-start(f32[432,128]{1,0:T(8,128)S(1)} %collective-permute-done.1.xhigh_ref) | copy-start | bytes 663556
  55.4 0.6 %copy-start.1 = (f32[16,8,128]{2,1,0:T(8,128)}, f32[16,8,128]{2,1,0:T(8,128)S(1)}, u32[]{:S(2)}) copy-start(f32[16,8,128]{2,1,0:T(8,128)S(1)} %all-to-all-done.1) | copy-start | bytes 196612
where the time goes:
time: 58.8 us; the launch traced here: 57.9 us
  Pallas kernels  32.4 us (55%)
  starting transfers between devices  19.8 us (34%)
  local copies, waits for them, and re-layouts  4.03 us (7%)
  waiting for transfers between devices  0.91 us (2%)
  between operations  0.72 us (1%)
    pallas_call x1, Pallas kernels, transport(): pl.pallas_call(transport_kernel, grid_spec=pltpu.PrefetchScalarGridSpec(n...  17.8 us
    all_to_all x1, starting transfers between devices, body(): on_air = exchange(to_air)  7.39 us
    all_to_all x1, starting transfers between devices, body(): on_sea = exchange(to_sea)  6.73 us
    pallas_call x1, Pallas kernels, edges(): pl.pallas_call(edges_kernel, grid_spec=pltpu.PrefetchScalarGridSpec(num_s...  6.66 us
    unnamed x16, local copies, waits for them, and re-layouts  4.03 us
    ppermute x1, starting transfers between devices, body(): xlow = lax.ppermute(high, 'gx', forward)  3.95 us
    pallas_call x1, Pallas kernels, air_send(): pl.pallas_call(air_send_kernel, grid=(1,), out_shape=(jax.ShapeDtypeStruc...  3.19 us
    pallas_call x1, Pallas kernels, sea_send(): pl.pallas_call(sea_send_kernel, grid=(1,), out_shape=jax.ShapeDtypeStruct...  2.78 us
  transfers between devices with their start and end apart: 5, of which 1 were waited for; matrix products, arithmetic and copies ran while one was open for 1% of the time, Pallas kernels for 48%

commit v1 on v0

--- a/solution.py
+++ b/solution.py
@@ -15,7 +15,15 @@
 
 time_step = 0.1
 diffusion = 0.2
-VMEM_LIMIT = 56 * 1024 * 1024
+VMEM_LIMIT = 32 * 1024 * 1024
+
+
+def held(array):
+    return pltpu.with_memory_space_constraint(array, pltpu.VMEM)
+
+
+def left(array):
+    return pltpu.with_memory_space_constraint(array, pltpu.HBM)
 
 
 def lane_of(shape):
@@ -52,7 +60,7 @@
         right = jnp.concatenate([weight_high, weight_low], axis=0)
         product = lax.dot_general(left, right, (((1,), (1,)), ((), ())), preferred_element_type=jnp.float32)
         total = product[:SUB, :WIN] + (product[SUB:, :WIN] + product[:SUB, WIN:])
-        d = dest_ref[k, 0]
+        d = dest_ref[k]
         slot = counts_ref[d]
         counts_ref[d] = slot + 1
         onehot = jnp.where(lane == window_ref[k], 1.0, 0.0)
@@ -111,7 +119,7 @@
         compiler_params=pltpu.CompilerParams(vmem_limit_bytes=VMEM_LIMIT),
         cost_estimate=pl.CostEstimate(flops=blocks * 2 * 16 * 128 * 256, bytes_accessed=2000000, transcendentals=0),
         name="sea_send",
-    )(dest, source, window, ocean, weights)
+    )(left(dest), left(source), left(window), left(ocean), left(weights))
 
 
 def air_send_kernel(
@@ -147,9 +155,9 @@
             smem,
             smem,
             smem,
-            pl.BlockSpec((tiles * CAP * ROWS, WIN), lambda i: (0, 0)),
+            pl.BlockSpec(memory_space=pltpu.VMEM),
             pl.BlockSpec((4, 1, rows, cols), lambda i: (0, 0, 0, 0)),
-            pl.BlockSpec(weights.shape, lambda i: (0, 0, 0)),
+            pl.BlockSpec(memory_space=pltpu.VMEM),
         ],
         out_specs=(
             pl.BlockSpec((tiles, CAP * ROWS, WIN), lambda i: (0, 0, 0)),
@@ -159,7 +167,7 @@
         compiler_params=pltpu.CompilerParams(vmem_limit_bytes=VMEM_LIMIT),
         cost_estimate=pl.CostEstimate(flops=blocks * 2 * 16 * 128 * 256, bytes_accessed=2000000, transcendentals=0),
         name="air_send",
-    )(dest, source, window, arrived.reshape(tiles * CAP * ROWS, WIN), atm, weights)
+    )(left(dest), left(source), left(window), held(arrived.reshape(tiles * CAP * ROWS, WIN)), left(atm), held(weights))
 
 
 def sea_forcing_kernel(arrived_ref, land_ref, before_ref, after_ref, summed_ref):
@@ -182,8 +190,8 @@
         grid=(1,),
         out_shape=jax.ShapeDtypeStruct(sea_next.shape, jnp.float32),
         in_specs=[
-            pl.BlockSpec((tiles * CAP * ROWS, WIN), lambda i: (0, 0)),
-            pl.BlockSpec((rows, cols), lambda i: (0, 0)),
+            pl.BlockSpec(memory_space=pltpu.VMEM),
+            pl.BlockSpec(memory_space=pltpu.VMEM),
             pl.BlockSpec((2, 1, rows, cols), lambda i: (0, 0, 0, 0)),
         ],
         out_specs=pl.BlockSpec((2, 1, rows, cols), lambda i: (0, 0, 0, 0)),
@@ -192,97 +200,99 @@
         compiler_params=pltpu.CompilerParams(vmem_limit_bytes=VMEM_LIMIT),
         cost_estimate=pl.CostEstimate(flops=4000000, bytes_accessed=600000, transcendentals=0),
         name="sea_forcing",
-    )(arrived.reshape(tiles * CAP * ROWS, WIN), land, sea_next)
-
-
-STEPS = 5
+    )(held(arrived.reshape(tiles * CAP * ROWS, WIN)), held(land), sea_next)
 
 
 def padded_levels(levels):
     return -(-levels // SUB) * SUB
 
 
-def edges_kernel(gy_ref, atm_ref, half_q_ref, half_v_ref, low_ref, high_ref, xlow_ref, xhigh_ref, y_ref):
-    step = pl.program_id(0)
+CHUNKS = 2
+
+
+def edges_kernel(gy_ref, atm_ref, ocean_ref, xlow_ref, xhigh_ref, y_ref, air, sea, sea_v, low, high, sems):
     air_levels, air_rows = atm_ref.shape[1:3]
-    sea_levels, sea_rows = half_q_ref.shape[1:3]
-    all_air, all_sea = air_levels * STEPS, sea_levels * STEPS
-    halves = low_ref.shape[3] // WIN
-    pitch = padded_levels(all_air)
-
-    @pl.when(step == 0)
-    def _():
-        xlow_ref[...] = jnp.zeros_like(xlow_ref)
-        xhigh_ref[...] = jnp.zeros_like(xhigh_ref)
-        y_ref[...] = jnp.zeros_like(y_ref)
-
+    sea_levels, sea_rows, sea_cols = ocean_ref.shape[1:]
+    halves = sea_cols // WIN
+    pitch = padded_levels(air_levels)
+    edge = jnp.where(gy_ref[0] == 0, LANES - 1, 0)
+    span = pl.ds(pl.multiple_of(jnp.where(gy_ref[0] == 0, sea_cols - LANES, 0), LANES), LANES)
+
+    def copies(chunk):
+        a = pl.ds(chunk * (air_levels // CHUNKS), air_levels // CHUNKS)
+        o = pl.ds(chunk * (sea_levels // CHUNKS), sea_levels // CHUNKS)
+        pairs = [
+            (atm_ref.at[:, a], air.at[:, a]),
+            (ocean_ref.at[pl.ds(0, 2), o, :, span], sea.at[:, o]),
+            (ocean_ref.at[3, o, :, span], sea_v.at[o]),
+            (ocean_ref.at[pl.ds(0, 3), o, pl.ds(0, SUB)], low.at[:, o]),
+            (ocean_ref.at[pl.ds(0, 3), o, pl.ds(sea_rows - SUB, SUB)], high.at[:, o]),
+        ]
+        return [pltpu.make_async_copy(src, dst, sems.at[chunk, i]) for i, (src, dst) in enumerate(pairs)]
+
+    for chunk in range(CHUNKS):
+        for copy in copies(chunk):
+            copy.start()
     for f in range(3):
-        for level in range(air_levels):
-            to = pl.ds(f * pitch + step * air_levels + level, 1)
-            xlow_ref[to, :] = atm_ref[f, level, pl.ds(0, 1), :]
-            xhigh_ref[to, :] = atm_ref[f, level, pl.ds(air_rows - 1, 1), :]
-        for h in range(halves):
-            for level in range(sea_levels):
-                to = pl.ds(3 * pitch + (f * halves + h) * all_sea + step * sea_levels + level, 1)
-                span = pl.ds(h * WIN, WIN)
-                xlow_ref[to, :] = low_ref[f, level, pl.ds(0, 1), span]
-                xhigh_ref[to, :] = high_ref[f, level, pl.ds(SUB - 1, 1), span]
-
-    edge = jnp.where(gy_ref[0] == 0, LANES - 1, 0)
+        for ref in (xlow_ref, xhigh_ref):
+            ref[pl.ds((f + 1) * pitch - SUB, SUB), :] = jnp.zeros((SUB, LANES), jnp.float32)
 
     def put(total, column, to, lane):
         return jnp.where(lane == to, pltpu.roll(column, (to - edge + LANES) % LANES, 1), total)
 
-    lane = lane_of((air_rows, LANES))
-    tracers, v = y_ref[:air_rows], y_ref[air_rows : 2 * air_rows]
-    for level in range(air_levels):
-        to = step * air_levels + level
-        tracers = put(tracers, atm_ref[0, level], to, lane)
-        tracers = put(tracers, atm_ref[1, level], LANES // 2 + to, lane)
-        v = put(v, atm_ref[3, level], to, lane)
+    air_lane, sea_lane = lane_of((air_rows, LANES)), lane_of((sea_rows, LANES))
+    tracers = v = jnp.zeros((air_rows, LANES), jnp.float32)
+    total = jnp.zeros((sea_rows, LANES), jnp.float32)
+    for chunk in range(CHUNKS):
+        for copy in copies(chunk):
+            copy.wait()
+        for level in range(chunk * (air_levels // CHUNKS), (chunk + 1) * (air_levels // CHUNKS)):
+            tracers = put(tracers, air[0, level], level, air_lane)
+            tracers = put(tracers, air[1, level], LANES // 2 + level, air_lane)
+            v = put(v, air[3, level], level, air_lane)
+            for f in range(3):
+                to = pl.ds(f * pitch + level, 1)
+                xlow_ref[to, :] = air[f, level, pl.ds(0, 1), :]
+                xhigh_ref[to, :] = air[f, level, pl.ds(air_rows - 1, 1), :]
+        for level in range(chunk * (sea_levels // CHUNKS), (chunk + 1) * (sea_levels // CHUNKS)):
+            total = put(total, sea[0, level], level, sea_lane)
+            total = put(total, sea[1, level], sea_levels + level, sea_lane)
+            total = put(total, sea_v[level], 2 * sea_levels + level, sea_lane)
+            for f in range(3):
+                for h in range(halves):
+                    to = pl.ds(3 * pitch + (f * halves + h) * sea_levels + level, 1)
+                    xlow_ref[to, :] = low[f, level, pl.ds(0, 1), pl.ds(h * WIN, WIN)]
+                    xhigh_ref[to, :] = high[f, level, pl.ds(SUB - 1, 1), pl.ds(h * WIN, WIN)]
     y_ref[:air_rows] = tracers
     y_ref[air_rows : 2 * air_rows] = v
-    lane = lane_of((sea_rows, LANES))
-    total = y_ref[2 * air_rows :]
-    for level in range(sea_levels):
-        to = step * sea_levels + level
-        total = put(total, half_q_ref[0, level], to, lane)
-        total = put(total, half_q_ref[1, level], all_sea + to, lane)
-        total = put(total, half_v_ref[0, level], 2 * all_sea + to, lane)
     y_ref[2 * air_rows :] = total
 
 
 def edges(gy, atm, ocean):
     air_levels, air_rows, _ = atm.shape[1:]
     sea_levels, sea_rows, sea_cols = ocean.shape[1:]
-    a, o = air_levels // STEPS, sea_levels // STEPS
     xrows = 3 * padded_levels(air_levels) + 3 * sea_levels * (sea_cols // WIN)
     yrows = 2 * air_rows + sea_rows
-    last = sea_cols // WIN - 1
     x_shape = jax.ShapeDtypeStruct((xrows, LANES), jnp.float32)
+    vmem = pl.BlockSpec(memory_space=pltpu.VMEM)
+    hbm = pl.BlockSpec(memory_space=pl.ANY)
     return pl.pallas_call(
         edges_kernel,
-        grid_spec=pltpu.PrefetchScalarGridSpec(
-            num_scalar_prefetch=1,
-            grid=(STEPS,),
-            in_specs=[
-                pl.BlockSpec((4, a, air_rows, LANES), lambda i, gy: (0, i, 0, 0)),
-                pl.BlockSpec((2, o, sea_rows, LANES), lambda i, gy: (0, i, 0, last * (1 - gy[0]))),
-                pl.BlockSpec((1, o, sea_rows, LANES), lambda i, gy: (3, i, 0, last * (1 - gy[0]))),
-                pl.BlockSpec((3, o, SUB, sea_cols), lambda i, gy: (0, i, 0, 0)),
-                pl.BlockSpec((3, o, SUB, sea_cols), lambda i, gy: (0, i, sea_rows // SUB - 1, 0)),
-            ],
-            out_specs=[
-                pl.BlockSpec((xrows, LANES), lambda i, gy: (0, 0)),
-                pl.BlockSpec((xrows, LANES), lambda i, gy: (0, 0)),
-                pl.BlockSpec((yrows, LANES), lambda i, gy: (0, 0)),
-            ],
-        ),
+        in_specs=[pl.BlockSpec(memory_space=pltpu.SMEM), hbm, hbm],
+        out_specs=[vmem, vmem, vmem],
         out_shape=(x_shape, x_shape, jax.ShapeDtypeStruct((yrows, LANES), jnp.float32)),
+        scratch_shapes=[
+            pltpu.VMEM(atm.shape, jnp.float32),
+            pltpu.VMEM((2, sea_levels, sea_rows, LANES), jnp.float32),
+            pltpu.VMEM((sea_levels, sea_rows, LANES), jnp.float32),
+            pltpu.VMEM((3, sea_levels, SUB, sea_cols), jnp.float32),
+            pltpu.VMEM((3, sea_levels, SUB, sea_cols), jnp.float32),
+            pltpu.SemaphoreType.DMA((CHUNKS, 5)),
+        ],
         compiler_params=pltpu.CompilerParams(vmem_limit_bytes=VMEM_LIMIT),
         cost_estimate=pl.CostEstimate(flops=2000000, bytes_accessed=10000000, transcendentals=0),
         name="edges",
-    )(gy, atm, ocean, ocean, ocean, ocean)
+    )(gy, left(atm), left(ocean))
 
 
 def step_level(fields, west, east, south, write):
@@ -344,12 +354,16 @@
         return self.ref[f, self.level, pl.ds(r * SUB, SUB), pl.ds(h * LANES, LANES)]
 
 
+STEPS = 5
+AIR_UNROLL = 12
+SEA_UNROLL = 8
+
+
 def transport_kernel(gy_ref, atm_ref, ocean_ref, land_ref, flux_ref, xlow_ref, xhigh_ref, y_ref, air_ref, sea_ref):
     step = pl.program_id(0)
-    steps = pl.num_programs(0)
     air_levels, air_rows = atm_ref.shape[1:3]
     sea_levels, sea_rows, sea_cols = ocean_ref.shape[1:]
-    all_air, all_sea = STEPS_T * air_levels, STEPS_T * sea_levels
+    all_air, all_sea = STEPS * air_levels, STEPS * sea_levels
     halves = sea_cols // LANES
     pitch = padded_levels(all_air)
     edge = jnp.where(gy_ref[0] == 0, LANES - 1, 0)
@@ -359,15 +373,17 @@
         tile = y_ref[pl.ds(start + r * SUB, SUB), :]
         return jnp.where(at_edge, pltpu.roll(tile, (edge - at + LANES) % LANES, 1), 0.0)
 
-    def air_level(level, carry):
+    def air_level(level):
         here = step * air_levels + level
 
         def beyond(f, r):
             start = air_rows if f == 3 else 0
             return column(start, r, (LANES // 2 if f == 1 else 0) + here)
 
+        stores = []
+
         def write(f, r, h, new, q):
-            air_ref[f, level, pl.ds(r * SUB, SUB), :] = new
+            stores.append((f, level, pl.ds(r * SUB, SUB), new))
 
         step_level(
             Fields(atm_ref, level),
@@ -376,24 +392,34 @@
             beyond,
             write,
         )
+        return stores
+
+    def some_air(i, carry):
+        stores = []
+        for level in range(AIR_UNROLL):
+            stores += air_level(i * AIR_UNROLL + level)
+        for *place, new in stores:
+            air_ref[tuple(place)] = new
         return carry
 
-    lax.fori_loop(0, air_levels, air_level, 0)
+    lax.fori_loop(0, air_levels // AIR_UNROLL, some_air, 0)
 
     @pl.when(step == 0)
     def _():
         for f in range(2):
             air_ref[f, 0] = air_ref[f, 0] + time_step * flux_ref[f]
 
-    def sea_level(level, carry):
+    def sea_level(level):
         here = step * sea_levels + level
 
         def beyond(f, r):
             return column(2 * air_rows, r, (2 if f == 3 else f) * all_sea + here)
 
+        stores = []
+
         def write(f, r, h, new, q):
             rows, span = pl.ds(r * SUB, SUB), pl.ds(h * LANES, LANES)
-            sea_ref[f, level, rows, span] = jnp.where(land_ref[rows, span] == 1, new, q)
+            stores.append((f, level, rows, span, jnp.where(land_ref[rows, span] == 1, new, q)))
 
         step_level(
             Fields(ocean_ref, level),
@@ -402,41 +428,37 @@
             beyond,
             write,
         )
+        return stores
+
+    def some_sea(i, carry):
+        stores = []
+        for level in range(SEA_UNROLL):
+            stores += sea_level(i * SEA_UNROLL + level)
+        for *place, new in stores:
+            sea_ref[tuple(place)] = new
         return carry
 
-    lax.fori_loop(0, sea_levels, sea_level, 0)
-
-
-STEPS_T = 10
+    lax.fori_loop(0, sea_levels // SEA_UNROLL, some_sea, 0)
 
 
 def transport(gy, atm, ocean, land, flux, xlow, xhigh, y):
     air_levels, air_rows, _ = atm.shape[1:]
     sea_levels, sea_rows, sea_cols = ocean.shape[1:]
-    a, o = air_levels // STEPS_T, sea_levels // STEPS_T
-
-    def whole(array):
-        return pl.BlockSpec(array.shape, lambda i, gy: (0,) * array.ndim)
-
+    a, o = air_levels // STEPS, sea_levels // STEPS
+    vmem = pl.BlockSpec(memory_space=pltpu.VMEM)
     return pl.pallas_call(
         transport_kernel,
-        grid_spec=pltpu.PrefetchScalarGridSpec(
-            num_scalar_prefetch=1,
-            grid=(STEPS_T,),
-            in_specs=[
-                pl.BlockSpec((4, a, air_rows, LANES), lambda i, gy: (0, i, 0, 0)),
-                pl.BlockSpec((4, o, sea_rows, sea_cols), lambda i, gy: (0, i, 0, 0)),
-                whole(land),
-                whole(flux),
-                whole(xlow),
-                whole(xhigh),
-                whole(y),
-            ],
-            out_specs=[
-                pl.BlockSpec((2, a, air_rows, LANES), lambda i, gy: (0, i, 0, 0)),
-                pl.BlockSpec((2, o, sea_rows, sea_cols), lambda i, gy: (0, i, 0, 0)),
-            ],
-        ),
+        grid=(STEPS,),
+        in_specs=[
+            pl.BlockSpec(memory_space=pltpu.SMEM),
+            pl.BlockSpec((4, a, air_rows, LANES), lambda i: (0, i, 0, 0)),
+            pl.BlockSpec((4, o, sea_rows, sea_cols), lambda i: (0, i, 0, 0)),
+        ]
+        + [vmem] * 5,
+        out_specs=[
+            pl.BlockSpec((2, a, air_rows, LANES), lambda i: (0, i, 0, 0)),
+            pl.BlockSpec((2, o, sea_rows, sea_cols), lambda i: (0, i, 0, 0)),
+        ],
         out_shape=(
             jax.ShapeDtypeStruct((2,) + atm.shape[1:], jnp.float32),
             jax.ShapeDtypeStruct((2,) + ocean.shape[1:], jnp.float32),
@@ -444,7 +466,7 @@
         compiler_params=pltpu.CompilerParams(vmem_limit_bytes=VMEM_LIMIT),
         cost_estimate=pl.CostEstimate(flops=60000000, bytes_accessed=22000000, transcendentals=0),
         name="transport",
-    )(gy, atm, ocean, land, flux, xlow, xhigh, y)
+    )(gy, left(atm), left(ocean), held(land), held(flux), held(xlow), held(xhigh), held(y))
 
 
 def body(
@@ -468,13 +490,14 @@
     forward = [(i, i + 1) for i in range(width_x - 1)]
     backward = [(i + 1, i) for i in range(width_x - 1)]
 
-    to_air = sea_send(tiles, ocean_fields, sea_weights, sea_dest, sea_source, sea_window)
+    to_air = sea_send(tiles, ocean_fields, sea_weights, sea_dest.reshape(-1), sea_source, sea_window)
     on_air = exchange(to_air)
     low, high, side = edges(gy, atm_fields, ocean_fields)
     side = lax.ppermute(side, "gy", [(0, 1), (1, 0)])
     xlow = lax.ppermute(high, "gx", forward)
     xhigh = lax.ppermute(low, "gx", backward)
-    to_sea, fluxes = air_send(on_air, atm_fields, air_weights, air_dest, air_source, air_window)
+    on_air, side = lax.optimization_barrier((on_air, side))
+    to_sea, fluxes = air_send(on_air, atm_fields, air_weights, air_dest.reshape(-1), air_source, air_window)
     on_sea = exchange(to_sea)
     air_next, sea_next = transport(gy, atm_fields, ocean_fields, land_sea, fluxes, xlow, xhigh, side)
     sea_next = add_sea_forcing(on_sea, land_sea, sea_next)

time: 58.8 us -> 47.2 us (0.80)
  Pallas kernels: 32.4 us -> 25.3 us
  local copies, waits for them, and re-layouts: 4.03 us -> 0.01 us
    pallas_call x2, Pallas kernels: 24.5 us -> 18 us  [the longest x1 12.8 us: transport(): pl.pallas_call(transport_kernel, grid=(STEPS,), in_specs=[pl.BlockSpec(me...]
    unnamed x16 -> x4, local copies, waits for them, and re-layouts: 4.03 us -> 0.01 us
    pallas_call x1, Pallas kernels: 3.19 us -> 2.54 us  [air_send(): pl.pallas_call(air_send_kernel, grid=(1,), out_shape=(jax.ShapeDtypeStruc...]
  transfers between devices with their start and end apart: 5 -> 5, of which waited for: 1 -> 1; matrix products, arithmetic and copies ran while one was open for 1% -> 0% of each run, Pallas kernels for 48% -> 44%
where the time goes in v1:
time: 47.2 us; the launch traced here: 46.7 us
  Pallas kernels  25.3 us (54%)
  starting transfers between devices  19.4 us (41%)
  waiting for transfers between devices  1.25 us (3%)
  between operations  0.73 us (2%)
    pallas_call x1, Pallas kernels, transport(): pl.pallas_call(transport_kernel, grid=(STEPS,), in_specs=[pl.BlockSpec(me...  12.8 us
    all_to_all x1, starting transfers between devices, body(): on_air = exchange(to_air)  7.39 us
    all_to_all x1, starting transfers between devices, body(): on_sea = exchange(to_sea)  6.73 us
    pallas_call x1, Pallas kernels, edges(): pl.pallas_call(edges_kernel, in_specs=[pl.BlockSpec(memory_space=pltpu.SM...  5.23 us
    ppermute x1, starting transfers between devices, body(): xlow = lax.ppermute(high, 'gx', forward)  3.97 us
    pallas_call x1, Pallas kernels, sea_send(): pl.pallas_call(sea_send_kernel, grid=(1,), out_shape=jax.ShapeDtypeStruct...  2.81 us
    pallas_call x1, Pallas kernels, air_send(): pl.pallas_call(air_send_kernel, grid=(1,), out_shape=(jax.ShapeDtypeStruc...  2.54 us
    pallas_call x1, Pallas kernels, add_sea_forcing(): pl.pallas_call(sea_forcing_kernel, grid=(1,), out_shape=jax.ShapeDtypeStr...  1.89 us
  transfers between devices with their start and end apart: 5, of which 1 were waited for; matrix products, arithmetic and copies ran while one was open for 0% of the time, Pallas kernels for 44%

profile of v1, /device:TPU:0, one launch (start us, length us, event | category | flops | bytes accessed | tf_op | source)
XLA Modules:
  0.0 46.7 jit_solution(7429801808681466415)
XLA Ops:
  0.6 2.8 %sea_send.1 = f32[16,8,128]{2,1,0:T(8,128)} custom-call(s32[24]{0:T(128)} %bitcast.7, s32[24]{0:T(128)} %source_ref.2, s32[24]{0:T(128)} %window_ref.2, f32[4,40,64,256]{3,2,1,0:T(8,128)} %ocean_ref.5, f32[24,128,128]{2,1,0:T(8,128)} %weights_ref.2), custom_call_target="tpu_custom_call" | custom-call | flops 25165824 | bytes 2000000 | tf_op jit(solution)/shard_map/sea_send/pallas_call | solution.py:102
  3.4 7.4 %all-to-all-start = ((f32[16,8,128]{2,1,0:T(8,128)}), f32[16,8,128]{2,1,0:T(8,128)S(1)}, u32[]{:S(2)}, u32[]{:S(2)}) async-start(f32[16,8,128]{2,1,0:T(8,128)} %sea_send.1), calls=%async_computation | async-start | bytes 131072 | tf_op jit(solution)/shard_map/all_to_all | solution.py:494
  10.8 0.0 copy-start
  10.8 5.2 %edges.1 = (f32[432,128]{1,0:T(8,128)S(1)}, f32[432,128]{1,0:T(8,128)S(1)}, f32[128,128]{1,0:T(8,128)S(1)}) custom-call(s32[1]{0:T(128)} %bitcast.gy_ref, f32[4,60,32,128]{3,2,1,0:T(8,128)} %atm_ref.5, f32[4,40,64,256]{3,2,1,0:T(8,128)} %ocean_ref.5), custom_call_target="tpu_custom_call" | custom-call | flops 2000000 | bytes 10000000 | tf_op jit(solution)/shard_map/edges/pallas_call | solution.py:279
  16.1 0.0 copy-start.1
  16.1 4.0 %collective-permute-start.1 = (f32[432,128]{1,0:T(8,128)S(1)}, f32[432,128]{1,0:T(8,128)S(1)}, u32[]{:S(2)}, u32[]{:S(2)}) collective-permute-start(f32[432,128]{1,0:T(8,128)S(1)} %get-tuple-element.14), channel_id=1, source_target_pairs={{0,2},{2,4},{4,6},{6,8},{8,10},{10,12},{12,14},{1,3},{3,5},{5,7},{... | collective-permute-start | bytes 663560 | tf_op jit(solution)/shard_map/ppermute | solution.py:497
  20.1 1.3 %collective-permute-start.2 = (f32[432,128]{1,0:T(8,128)S(1)}, f32[432,128]{1,0:T(8,128)S(1)}, u32[]{:S(2)}, u32[]{:S(2)}) collective-permute-start(f32[432,128]{1,0:T(8,128)S(1)} %get-tuple-element.15), channel_id=1, source_target_pairs={{2,0},{4,2},{6,4},{8,6},{10,8},{12,10},{14,12},{3,1},{5,3},{7,5},{... | collective-permute-start | bytes 663560 | tf_op jit(solution)/shard_map/ppermute | solution.py:498
  21.4 0.1 collective-permute-start
  21.5 1.2 %collective-permute-done.y_ref = f32[128,128]{1,0:T(8,128)S(1)} collective-permute-done((f32[128,128]{1,0:T(8,128)S(1)}, f32[128,128]{1,0:T(8,128)S(1)}, u32[]{:S(2)}, u32[]{:S(2)}) %collective-permute-start) | collective-permute-done | bytes 65568 | tf_op jit(solution)/shard_map/ppermute | solution.py:496
  22.7 0.0 all-to-all-done
  22.7 0.0 copy-done
  22.7 2.5 %air_send.1 = (f32[16,8,128]{2,1,0:T(8,128)}, f32[2,32,128]{2,1,0:T(8,128)S(1)}) custom-call(s32[24]{0:T(128)} %bitcast.8, s32[24]{0:T(128)} %source_ref.3, s32[24]{0:T(128)} %window_ref.3, f32[128,128]{1,0:T(8,128)S(1)} %bitcast.5, f32[4,60,32,128]{3,2,1,0:T(8,128)} %atm_ref.5, f32[24,128,128]{2,1,0:T(8,128)S(1)} %copy-done), custom_call_target="tpu_custom_call" | custom-call | flops 25165824 | bytes 2000000 | tf_op jit(solution)/shard_map/air_send/pallas_call | solution.py:147
  25.2 6.7 %all-to-all-start.1 = ((f32[16,8,128]{2,1,0:T(8,128)}), f32[16,8,128]{2,1,0:T(8,128)S(1)}, u32[]{:S(2)}, u32[]{:S(2)}) async-start(f32[16,8,128]{2,1,0:T(8,128)} %get-tuple-element.18), calls=%async_computation.1 | async-start | bytes 131072 | tf_op jit(solution)/shard_map/all_to_all | solution.py:501
  32.0 0.0 collective-permute-done.1.xlow_ref
  32.0 0.0 collective-permute-done.2.xhigh_ref
  32.0 0.0 copy-done.1
  32.0 12.8 %transport.1 = (f32[2,60,32,128]{3,2,1,0:T(8,128)}, f32[2,40,64,256]{3,2,1,0:T(8,128)}) custom-call(s32[1]{0:T(128)} %bitcast.gy_ref, f32[4,60,32,128]{3,2,1,0:T(8,128)} %atm_ref.5, f32[4,40,64,256]{3,2,1,0:T(8,128)} %ocean_ref.5, s32[64,256]{1,0:T(8,128)S(1)} %copy-done.1, f32[2,32,128]{2,1,0:T(8,128)S(1)} %get-tuple-element.13.flux_ref, ...), custom_call_target="tpu_custom_call" | custom-call | flops 60000000 | bytes 22000000 | tf_op jit(solution)/shard_map/transport/pallas_call | solution.py:449
  44.8 0.0 all-to-all-done.1
  44.8 1.9 %sea_forcing.1 = f32[2,40,64,256]{3,2,1,0:T(8,128)} custom-call(f32[128,128]{1,0:T(8,128)S(1)} %bitcast.6, s32[64,256]{1,0:T(8,128)S(1)} %copy-done.1, f32[2,40,64,256]{3,2,1,0:T(8,128)} %get-tuple-element.19.before_ref), custom_call_target="tpu_custom_call", output_to_operand_aliasing={{}: (2, {})} | custom-call | flops 4000000 | bytes 600000 | tf_op jit(solution)/shard_map/sea_forcing/pallas_call | solution.py:188
Async XLA Ops:
  3.4 19.3 %all-to-all-start = ((f32[16,8,128]{2,1,0:T(8,128)}), f32[16,8,128]{2,1,0:T(8,128)S(1)}, u32[]{:S(2)}, u32[]{:S(2)}) async-start(f32[16,8,128]{2,1,0:T(8,128)} %sea_send.1), calls=%async_computation | async-start | bytes 131072 | tf_op jit(solution)/shard_map/all_to_all | solution.py:494
  10.8 11.9 %copy-start = (f32[24,128,128]{2,1,0:T(8,128)S(1)}, f32[24,128,128]{2,1,0:T(8,128)}, u32[]{:S(2)}) copy-start(f32[24,128,128]{2,1,0:T(8,128)} %weights_ref.3) | copy-start | bytes 4718596
  16.1 15.9 %copy-start.1 = (s32[64,256]{1,0:T(8,128)S(1)}, s32[64,256]{1,0:T(8,128)}, u32[]{:S(2)}) copy-start(s32[64,256]{1,0:T(8,128)} %land_ref.3) | copy-start | bytes 196612
  16.1 15.9 %collective-permute-start.1 = (f32[432,128]{1,0:T(8,128)S(1)}, f32[432,128]{1,0:T(8,128)S(1)}, u32[]{:S(2)}, u32[]{:S(2)}) collective-permute-start(f32[432,128]{1,0:T(8,128)S(1)} %get-tuple-element.14), channel_id=1, source_target_pairs={{0,2},{2,4},{4,6},{6,8},{8,10},{10,12},{12,14},{1,3},{3,5},{5,7},{... | collective-permute-start | bytes 663560 | tf_op jit(solution)/shard_map/ppermute | solution.py:497
  20.1 11.9 %collective-permute-start.2 = (f32[432,128]{1,0:T(8,128)S(1)}, f32[432,128]{1,0:T(8,128)S(1)}, u32[]{:S(2)}, u32[]{:S(2)}) collective-permute-start(f32[432,128]{1,0:T(8,128)S(1)} %get-tuple-element.15), channel_id=1, source_target_pairs={{2,0},{4,2},{6,4},{8,6},{10,8},{12,10},{14,12},{3,1},{5,3},{7,5},{... | collective-permute-start | bytes 663560 | tf_op jit(solution)/shard_map/ppermute | solution.py:498
  21.4 1.3 %collective-permute-start = (f32[128,128]{1,0:T(8,128)S(1)}, f32[128,128]{1,0:T(8,128)S(1)}, u32[]{:S(2)}, u32[]{:S(2)}) collective-permute-start(f32[128,128]{1,0:T(8,128)S(1)} %get-tuple-element.11), channel_id=1, source_target_pairs={{0,1},{1,0},{2,3},{3,2},{4,5},{5,4},{6,7},{7,6},{8,9},{9,8},{10,11... | collective-permute-start | bytes 196616 | tf_op jit(solution)/shard_map/ppermute | solution.py:496
  25.2 19.6 %all-to-all-start.1 = ((f32[16,8,128]{2,1,0:T(8,128)}), f32[16,8,128]{2,1,0:T(8,128)S(1)}, u32[]{:S(2)}, u32[]{:S(2)}) async-start(f32[16,8,128]{2,1,0:T(8,128)} %get-tuple-element.18), calls=%async_computation.1 | async-start | bytes 131072 | tf_op jit(solution)/shard_map/all_to_all | solution.py:501

commit v2 on v1

--- a/solution.py
+++ b/solution.py
@@ -15,7 +15,7 @@
 
 time_step = 0.1
 diffusion = 0.2
-VMEM_LIMIT = 32 * 1024 * 1024
+VMEM_LIMIT = 40 * 1024 * 1024
 
 
 def held(array):
@@ -295,178 +295,219 @@
     )(gy, left(atm), left(ocean))
 
 
-def step_level(fields, west, east, south, write):
-    row = row_of((SUB, LANES))
+STEPS = 5
+PAD = 8
+
+
+def beyond_columns(gy, mine, v_mine, other, v_other):
+    scale, mixing = 0.25 * time_step, time_step * diffusion
+    sign = jnp.where(gy == 0, -scale, scale)
+    return mixing * other + sign * ((v_mine + v_other) * other + v_other * mine)
+
+
+def step_level(ref, index, groups, halves, beyond, write):
     lane = lane_of((SUB, LANES))
-    groups, halves = fields.groups, fields.halves
-    first_row, last_row = row == 0, row == SUB - 1
     first_lane, last_lane = lane == 0, lane == LANES - 1
-
-    def along_x(f, h, scale):
-        tiles = [fields(f, r, h) for r in range(groups)]
-        if scale is not None:
-            tiles = [scale * t for t in tiles]
-        down = [pltpu.roll(t, 1, 0) for t in tiles]
-        up = [pltpu.roll(t, SUB - 1, 0) for t in tiles]
-        before = [jnp.broadcast_to(west(f, h), (SUB, LANES))] + down[:-1]
-        after = up[1:] + [jnp.broadcast_to(east(f, h), (SUB, LANES))]
-        if scale is not None:
-            before[0], after[-1] = scale * before[0], scale * after[-1]
-        lows = [jnp.where(first_row, b, d) for b, d in zip(before, down)]
-        highs = [jnp.where(last_row, a, u) for a, u in zip(after, up)]
-        return tiles, lows, highs
-
-    def along_y(f, r, tiles, scale):
-        beyond = south(f, r)
-        if scale is not None:
-            beyond = scale * beyond
+    scale, mixing = 0.25 * time_step, time_step * diffusion
+
+    def rows(f, h, r, offset):
+        return ref[index(f, h) + (pl.ds(PAD + r * SUB + offset, SUB), slice(None))]
+
+    def along_y(tiles):
         right = [pltpu.roll(t, 1, 1) for t in tiles]
         left = [pltpu.roll(t, LANES - 1, 1) for t in tiles]
-        lows = [jnp.where(first_lane, b, t) for b, t in zip([beyond] + right[:-1], right)]
-        highs = [jnp.where(last_lane, b, t) for b, t in zip(left[1:] + [beyond], left)]
+        lows = [jnp.where(first_lane, b, t) for b, t in zip([0.0] + right[:-1], right)]
+        highs = [jnp.where(last_lane, b, t) for b, t in zip(left[1:] + [0.0], left)]
         return lows, highs
 
-    scale = 0.25 * time_step
-    mixing = time_step * diffusion
-    moved = [[along_x(f, h, scale if f == 2 else None) for h in range(halves)] for f in range(3)]
     for r in range(groups):
-        v = [scale * fields(3, r, h) for h in range(halves)]
-        v_low, v_high = along_y(3, r, v, scale)
-        sides = [along_y(f, r, [moved[f][h][0][r] for h in range(halves)], None) for f in range(2)]
+        q = [[rows(f, h, r, 0) for h in range(halves)] for f in range(2)]
+        v = [scale * rows(3, h, r, 0) for h in range(halves)]
+        v_low, v_high = along_y(v)
+        sides = [along_y(q[f]) for f in range(2)]
         for h in range(halves):
-            u, u_low, u_high = (part[r] for part in moved[2][h])
+            u, u_low, u_high = (scale * rows(2, h, r, offset) for offset in (0, -1, 1))
             centre = (1.0 - 4.0 * mixing) + ((u_low - u_high) + (v_low[h] - v_high[h]))
             x_high, x_low = (mixing - u) - u_high, (mixing + u) + u_low
             y_high, y_low = (mixing - v[h]) - v_high[h], (mixing + v[h]) + v_low[h]
             for f in range(2):
-                q, q_low, q_high = (part[r] for part in moved[f][h])
-                new = centre * q + (x_high * q_high + x_low * q_low)
+                new = centre * q[f][h] + (x_high * rows(f, h, r, 1) + x_low * rows(f, h, r, -1))
                 new = new + (y_high * sides[f][1][h] + y_low * sides[f][0][h])
-                write(f, r, h, new, q)
-
-
-class Fields:
-    def __init__(self, ref, level):
-        self.ref, self.level = ref, level
-        self.groups, self.halves = ref.shape[2] // SUB, ref.shape[3] // LANES
-
-    def __call__(self, f, r, h):
-        return self.ref[f, self.level, pl.ds(r * SUB, SUB), pl.ds(h * LANES, LANES)]
-
-
-STEPS = 5
-AIR_UNROLL = 12
-SEA_UNROLL = 8
-
-
-def transport_kernel(gy_ref, atm_ref, ocean_ref, land_ref, flux_ref, xlow_ref, xhigh_ref, y_ref, air_ref, sea_ref):
-    step = pl.program_id(0)
-    air_levels, air_rows = atm_ref.shape[1:3]
-    sea_levels, sea_rows, sea_cols = ocean_ref.shape[1:]
-    all_air, all_sea = STEPS * air_levels, STEPS * sea_levels
+                write(f, r, h, new + beyond(f, r, h), q[f][h])
+
+
+def transport_kernel(
+    gy_ref,
+    atm_ref,
+    ocean_ref,
+    land_ref,
+    flux_ref,
+    xlow_ref,
+    xhigh_ref,
+    mine_ref,
+    y_ref,
+    air_ref,
+    sea_ref,
+    air,
+    sea,
+    air_new,
+    sea_new,
+    air_edge,
+    sea_edge,
+    in_sems,
+    out_sems,
+):
+    all_air, air_rows = atm_ref.shape[1:3]
+    all_sea, sea_rows, sea_cols = ocean_ref.shape[1:]
+    a, o = all_air // STEPS, all_sea // STEPS
     halves = sea_cols // LANES
     pitch = padded_levels(all_air)
-    edge = jnp.where(gy_ref[0] == 0, LANES - 1, 0)
-    at_edge = lane_of((SUB, LANES)) == edge
-
-    def column(start, r, at):
-        tile = y_ref[pl.ds(start + r * SUB, SUB), :]
-        return jnp.where(at_edge, pltpu.roll(tile, (edge - at + LANES) % LANES, 1), 0.0)
-
-    def air_level(level):
-        here = step * air_levels + level
-
-        def beyond(f, r):
-            start = air_rows if f == 3 else 0
-            return column(start, r, (LANES // 2 if f == 1 else 0) + here)
-
+    gy = gy_ref[0]
+
+    def air_in(step):
+        levels = pl.ds(step * a, a)
+        yield pltpu.make_async_copy(
+            atm_ref.at[:, levels], air.at[:, levels, pl.ds(PAD, air_rows)], in_sems.at[step, halves]
+        )
+
+    def sea_in(step):
+        levels = pl.ds(step * o, o)
+        for h in range(halves):
+            yield pltpu.make_async_copy(
+                ocean_ref.at[:, levels, :, pl.ds(h * LANES, LANES)],
+                sea.at[h, :, levels, pl.ds(PAD, sea_rows)],
+                in_sems.at[step, h],
+            )
+
+    def air_out(step):
+        levels = pl.ds(step * a, a)
+        return pltpu.make_async_copy(air_new.at[:, levels], air_ref.at[:, levels], out_sems.at[step, 0])
+
+    def sea_out(step):
+        levels = pl.ds(step * o, o)
+        return pltpu.make_async_copy(sea_new.at[:, levels], sea_ref.at[:, levels], out_sems.at[step, 1])
+
+    for step in range(STEPS):
+        for copy in (*air_in(step), *sea_in(step)):
+            copy.start()
+
+    lane = lane_of((air_rows, LANES))
+    mine, other = mine_ref[:air_rows], y_ref[:air_rows]
+
+    def twice(v):
+        return jnp.where(lane < LANES // 2, v, pltpu.roll(v, LANES // 2, 1))
+
+    v_mine, v_other = twice(mine_ref[air_rows : 2 * air_rows]), twice(y_ref[air_rows : 2 * air_rows])
+    air_edge[...] = beyond_columns(gy, mine, v_mine, other, v_other)
+    lane = lane_of((sea_rows, LANES))
+    mine, other = mine_ref[2 * air_rows :], y_ref[2 * air_rows :]
+
+    def both(columns):
+        first, second = (pltpu.roll(columns, LANES - n * all_sea, 1) for n in (2, 1))
+        return jnp.where(lane < all_sea, first, second)
+
+    sea_edge[...] = beyond_columns(gy, mine, both(mine), other, both(other))
+
+    edge = jnp.where(gy == 0, LANES - 1, 0)
+    lane = lane_of((SUB, LANES))
+    at_first, at_last = (lane == 0) & (gy != 0), (lane == LANES - 1) & (gy == 0)
+    at_edge = lane == edge
+
+    def column(ref, r, at):
+        return pltpu.roll(ref[pl.ds(r * SUB, SUB), :], (edge - at + LANES) % LANES, 1)
+
+    def some_levels(step, carry):
+        for copy in air_in(step):
+            copy.wait()
+        for j in range(a):
+            level = step * a + j
+            for f in range(3):
+                air[f, level, pl.ds(PAD - 1, 1), :] = xlow_ref[pl.ds(f * pitch + level, 1), :]
+                air[f, level, pl.ds(PAD + air_rows, 1), :] = xhigh_ref[pl.ds(f * pitch + level, 1), :]
         stores = []
-
-        def write(f, r, h, new, q):
-            stores.append((f, level, pl.ds(r * SUB, SUB), new))
-
-        step_level(
-            Fields(atm_ref, level),
-            lambda f, h: xlow_ref[pl.ds(f * pitch + here, 1), :],
-            lambda f, h: xhigh_ref[pl.ds(f * pitch + here, 1), :],
-            beyond,
-            write,
-        )
-        return stores
-
-    def some_air(i, carry):
+        for j in range(a):
+            level = step * a + j
+
+            def beyond(f, r, h):
+                return jnp.where(at_edge, column(air_edge, r, f * (LANES // 2) + level), 0.0)
+
+            def write(f, r, h, new, q):
+                stores.append((f, level, pl.ds(r * SUB, SUB), new))
+
+            step_level(air, lambda f, h: (f, level), air_rows // SUB, 1, beyond, write)
+        for *place, new in stores:
+            air_new[tuple(place)] = new
+
+        @pl.when(step == 0)
+        def _():
+            for f in range(2):
+                air_new[f, 0] = air_new[f, 0] + time_step * flux_ref[f]
+
+        air_out(step).start()
+        for copy in sea_in(step):
+            copy.wait()
+        for j in range(o):
+            level = step * o + j
+            for f in range(3):
+                for h in range(halves):
+                    at = pl.ds(3 * pitch + (f * halves + h) * all_sea + level, 1)
+                    sea[h, f, level, pl.ds(PAD - 1, 1), :] = xlow_ref[at, :]
+                    sea[h, f, level, pl.ds(PAD + sea_rows, 1), :] = xhigh_ref[at, :]
         stores = []
-        for level in range(AIR_UNROLL):
-            stores += air_level(i * AIR_UNROLL + level)
+        for j in range(o):
+            level = step * o + j
+            columns = {}
+
+            def beyond(f, r, h):
+                if (f, r) not in columns:
+                    columns[f, r] = column(sea_edge, r, f * all_sea + level)
+                added = columns[f, r]
+                if h == 0:
+                    return jnp.where(at_first, added, 0.0)
+                return jnp.where(at_last, added, 0.0) if h == halves - 1 else 0.0
+
+            def write(f, r, h, new, q):
+                rows, span = pl.ds(r * SUB, SUB), pl.ds(h * LANES, LANES)
+                stores.append((f, level, rows, span, jnp.where(land_ref[rows, span] == 1, new, q)))
+
+            step_level(sea, lambda f, h: (h, f, level), sea_rows // SUB, halves, beyond, write)
         for *place, new in stores:
-            air_ref[tuple(place)] = new
+            sea_new[tuple(place)] = new
+        sea_out(step).start()
         return carry
 
-    lax.fori_loop(0, air_levels // AIR_UNROLL, some_air, 0)
-
-    @pl.when(step == 0)
-    def _():
-        for f in range(2):
-            air_ref[f, 0] = air_ref[f, 0] + time_step * flux_ref[f]
-
-    def sea_level(level):
-        here = step * sea_levels + level
-
-        def beyond(f, r):
-            return column(2 * air_rows, r, (2 if f == 3 else f) * all_sea + here)
-
-        stores = []
-
-        def write(f, r, h, new, q):
-            rows, span = pl.ds(r * SUB, SUB), pl.ds(h * LANES, LANES)
-            stores.append((f, level, rows, span, jnp.where(land_ref[rows, span] == 1, new, q)))
-
-        step_level(
-            Fields(ocean_ref, level),
-            lambda f, h: xlow_ref[pl.ds(3 * pitch + (f * halves + h) * all_sea + here, 1), :],
-            lambda f, h: xhigh_ref[pl.ds(3 * pitch + (f * halves + h) * all_sea + here, 1), :],
-            beyond,
-            write,
-        )
-        return stores
-
-    def some_sea(i, carry):
-        stores = []
-        for level in range(SEA_UNROLL):
-            stores += sea_level(i * SEA_UNROLL + level)
-        for *place, new in stores:
-            sea_ref[tuple(place)] = new
-        return carry
-
-    lax.fori_loop(0, sea_levels // SEA_UNROLL, some_sea, 0)
-
-
-def transport(gy, atm, ocean, land, flux, xlow, xhigh, y):
+    lax.fori_loop(0, STEPS, some_levels, 0)
+    for step in range(STEPS):
+        air_out(step).wait()
+        sea_out(step).wait()
+
+
+def transport(gy, atm, ocean, land, flux, xlow, xhigh, mine, y):
     air_levels, air_rows, _ = atm.shape[1:]
     sea_levels, sea_rows, sea_cols = ocean.shape[1:]
-    a, o = air_levels // STEPS, sea_levels // STEPS
+    halves = sea_cols // LANES
     vmem = pl.BlockSpec(memory_space=pltpu.VMEM)
+    hbm = pl.BlockSpec(memory_space=pltpu.HBM)
+    air_shape, sea_shape = (2,) + atm.shape[1:], (2,) + ocean.shape[1:]
     return pl.pallas_call(
         transport_kernel,
-        grid=(STEPS,),
-        in_specs=[
-            pl.BlockSpec(memory_space=pltpu.SMEM),
-            pl.BlockSpec((4, a, air_rows, LANES), lambda i: (0, i, 0, 0)),
-            pl.BlockSpec((4, o, sea_rows, sea_cols), lambda i: (0, i, 0, 0)),
-        ]
-        + [vmem] * 5,
-        out_specs=[
-            pl.BlockSpec((2, a, air_rows, LANES), lambda i: (0, i, 0, 0)),
-            pl.BlockSpec((2, o, sea_rows, sea_cols), lambda i: (0, i, 0, 0)),
+        in_specs=[pl.BlockSpec(memory_space=pltpu.SMEM), hbm, hbm] + [vmem] * 6,
+        out_specs=[hbm, hbm],
+        out_shape=(jax.ShapeDtypeStruct(air_shape, jnp.float32), jax.ShapeDtypeStruct(sea_shape, jnp.float32)),
+        scratch_shapes=[
+            pltpu.VMEM((4, air_levels, air_rows + 2 * PAD, LANES), jnp.float32),
+            pltpu.VMEM((halves, 4, sea_levels, sea_rows + 2 * PAD, LANES), jnp.float32),
+            pltpu.VMEM(air_shape, jnp.float32),
+            pltpu.VMEM(sea_shape, jnp.float32),
+            pltpu.VMEM((air_rows, LANES), jnp.float32),
+            pltpu.VMEM((sea_rows, LANES), jnp.float32),
+            pltpu.SemaphoreType.DMA((STEPS, halves + 1)),
+            pltpu.SemaphoreType.DMA((STEPS, 2)),
         ],
-        out_shape=(
-            jax.ShapeDtypeStruct((2,) + atm.shape[1:], jnp.float32),
-            jax.ShapeDtypeStruct((2,) + ocean.shape[1:], jnp.float32),
-        ),
         compiler_params=pltpu.CompilerParams(vmem_limit_bytes=VMEM_LIMIT),
         cost_estimate=pl.CostEstimate(flops=60000000, bytes_accessed=22000000, transcendentals=0),
         name="transport",
-    )(gy, left(atm), left(ocean), held(land), held(flux), held(xlow), held(xhigh), held(y))
+    )(gy, left(atm), left(ocean), held(land), held(flux), held(xlow), held(xhigh), held(mine), held(y))
 
 
 def body(
@@ -492,14 +533,14 @@
 
     to_air = sea_send(tiles, ocean_fields, sea_weights, sea_dest.reshape(-1), sea_source, sea_window)
     on_air = exchange(to_air)
-    low, high, side = edges(gy, atm_fields, ocean_fields)
-    side = lax.ppermute(side, "gy", [(0, 1), (1, 0)])
+    low, high, mine = edges(gy, atm_fields, ocean_fields)
+    side = lax.ppermute(mine, "gy", [(0, 1), (1, 0)])
     xlow = lax.ppermute(high, "gx", forward)
     xhigh = lax.ppermute(low, "gx", backward)
-    on_air, side = lax.optimization_barrier((on_air, side))
     to_sea, fluxes = air_send(on_air, atm_fields, air_weights, air_dest.reshape(-1), air_source, air_window)
+    to_sea, side = lax.optimization_barrier((to_sea, side))
     on_sea = exchange(to_sea)
-    air_next, sea_next = transport(gy, atm_fields, ocean_fields, land_sea, fluxes, xlow, xhigh, side)
+    air_next, sea_next = transport(gy, atm_fields, ocean_fields, land_sea, fluxes, xlow, xhigh, mine, side)
     sea_next = add_sea_forcing(on_sea, land_sea, sea_next)
     return (air_next, sea_next)
 

time: 47.2 us -> 43.3 us (0.917)
  Pallas kernels: 25.3 us -> 22.6 us
  waiting for transfers between devices: 1.25 us -> 0.01 us
    pallas_call x1, Pallas kernels: 12.8 us -> 10.1 us  [transport(): pl.pallas_call(transport_kernel, in_specs=[pl.BlockSpec(memory_space=pltp...]
    ppermute x1, waiting for transfers between devices: 1.24 us -> 0.01 us  [body(): side = lax.ppermute(mine, 'gy', [(0, 1), (1, 0)])]
  transfers between devices with their start and end apart: 5 -> 5, of which waited for: 1 -> 0; matrix products, arithmetic and copies ran while one was open for 0% -> 0% of each run, Pallas kernels for 44% -> 42%
where the time goes in v2:
time: 43.3 us; the launch traced here: 42.9 us
  Pallas kernels  22.6 us (52%)
  starting transfers between devices  19.5 us (45%)
  between operations  0.76 us (2%)
    pallas_call x1, Pallas kernels, transport(): pl.pallas_call(transport_kernel, in_specs=[pl.BlockSpec(memory_space=pltp...  10.1 us
    all_to_all x1, starting transfers between devices, body(): on_air = exchange(to_air)  7.39 us
    all_to_all x1, starting transfers between devices, body(): on_sea = exchange(to_sea)  6.81 us
    pallas_call x1, Pallas kernels, edges(): pl.pallas_call(edges_kernel, in_specs=[pl.BlockSpec(memory_space=pltpu.SM...  5.23 us
    ppermute x1, starting transfers between devices, body(): xlow = lax.ppermute(high, 'gx', forward)  3.97 us
    pallas_call x1, Pallas kernels, sea_send(): pl.pallas_call(sea_send_kernel, grid=(1,), out_shape=jax.ShapeDtypeStruct...  2.81 us
    pallas_call x1, Pallas kernels, air_send(): pl.pallas_call(air_send_kernel, grid=(1,), out_shape=(jax.ShapeDtypeStruc...  2.54 us
    pallas_call x1, Pallas kernels, add_sea_forcing(): pl.pallas_call(sea_forcing_kernel, grid=(1,), out_shape=jax.ShapeDtypeStr...  1.91 us
  transfers between devices with their start and end apart: 5, of which 0 were waited for; matrix products, arithmetic and copies ran while one was open for 0% of the time, Pallas kernels for 42%

profile of v2, /device:TPU:0, one launch (start us, length us, event | category | flops | bytes accessed | tf_op | source)
XLA Modules:
  0.0 42.9 jit_solution(7718348631738271275)
XLA Ops:
  0.6 2.8 %sea_send.1 = f32[16,8,128]{2,1,0:T(8,128)} custom-call(s32[24]{0:T(128)} %bitcast.7, s32[24]{0:T(128)} %source_ref.2, s32[24]{0:T(128)} %window_ref.2, f32[4,40,64,256]{3,2,1,0:T(8,128)} %ocean_ref.5, f32[24,128,128]{2,1,0:T(8,128)} %weights_ref.2), custom_call_target="tpu_custom_call" | custom-call | flops 25165824 | bytes 2000000 | tf_op jit(solution)/shard_map/sea_send/pallas_call | solution.py:102
  3.4 7.4 %all-to-all-start = ((f32[16,8,128]{2,1,0:T(8,128)}), f32[16,8,128]{2,1,0:T(8,128)S(1)}, u32[]{:S(2)}, u32[]{:S(2)}) async-start(f32[16,8,128]{2,1,0:T(8,128)} %sea_send.1), calls=%async_computation | async-start | bytes 131072 | tf_op jit(solution)/shard_map/all_to_all | solution.py:535
  10.8 0.0 copy-start
  10.8 5.2 %edges.1 = (f32[432,128]{1,0:T(8,128)S(1)}, f32[432,128]{1,0:T(8,128)S(1)}, f32[128,128]{1,0:T(8,128)S(1)}) custom-call(s32[1]{0:T(128)} %bitcast.gy_ref, f32[4,60,32,128]{3,2,1,0:T(8,128)} %atm_ref.5, f32[4,40,64,256]{3,2,1,0:T(8,128)} %ocean_ref.5), custom_call_target="tpu_custom_call" | custom-call | flops 2000000 | bytes 10000000 | tf_op jit(solution)/shard_map/edges/pallas_call | solution.py:279
  16.1 0.0 copy-start.1
  16.1 4.0 %collective-permute-start = (f32[432,128]{1,0:T(8,128)S(1)}, f32[432,128]{1,0:T(8,128)S(1)}, u32[]{:S(2)}, u32[]{:S(2)}) collective-permute-start(f32[432,128]{1,0:T(8,128)S(1)} %get-tuple-element.12), channel_id=1, source_target_pairs={{0,2},{2,4},{4,6},{6,8},{8,10},{10,12},{12,14},{1,3},{3,5},{5,7},{... | collective-permute-start | bytes 663560 | tf_op jit(solution)/shard_map/ppermute | solution.py:538
  20.1 1.3 %collective-permute-start.1 = (f32[432,128]{1,0:T(8,128)S(1)}, f32[432,128]{1,0:T(8,128)S(1)}, u32[]{:S(2)}, u32[]{:S(2)}) collective-permute-start(f32[432,128]{1,0:T(8,128)S(1)} %get-tuple-element.13), channel_id=1, source_target_pairs={{2,0},{4,2},{6,4},{8,6},{10,8},{12,10},{14,12},{3,1},{5,3},{7,5},{... | collective-permute-start | bytes 663560 | tf_op jit(solution)/shard_map/ppermute | solution.py:539
  21.4 0.1 collective-permute-start.2
  21.5 0.0 all-to-all-done
  21.5 0.0 copy-done
  21.5 2.5 %air_send.1 = (f32[16,8,128]{2,1,0:T(8,128)}, f32[2,32,128]{2,1,0:T(8,128)S(1)}) custom-call(s32[24]{0:T(128)} %bitcast.8, s32[24]{0:T(128)} %source_ref.3, s32[24]{0:T(128)} %window_ref.3, f32[128,128]{1,0:T(8,128)S(1)} %bitcast.5, f32[4,60,32,128]{3,2,1,0:T(8,128)} %atm_ref.5, f32[24,128,128]{2,1,0:T(8,128)S(1)} %copy-done), custom_call_target="tpu_custom_call" | custom-call | flops 25165824 | bytes 2000000 | tf_op jit(solution)/shard_map/air_send/pallas_call | solution.py:147
  24.0 0.0 collective-permute-done.2.y_ref
  24.0 6.8 %all-to-all-start.1 = ((f32[16,8,128]{2,1,0:T(8,128)}), f32[16,8,128]{2,1,0:T(8,128)S(1)}, u32[]{:S(2)}, u32[]{:S(2)}) async-start(f32[16,8,128]{2,1,0:T(8,128)} %get-tuple-element.18), calls=%async_computation.1 | async-start | bytes 131072 | tf_op jit(solution)/shard_map/all_to_all | solution.py:542
  30.8 0.0 collective-permute-done.xlow_ref
  30.8 0.0 collective-permute-done.1.xhigh_ref
  30.9 0.0 copy-done.1
  30.9 10.1 %transport.1 = (f32[2,60,32,128]{3,2,1,0:T(8,128)}, f32[2,40,64,256]{3,2,1,0:T(8,128)}) custom-call(s32[1]{0:T(128)} %bitcast.gy_ref, f32[4,60,32,128]{3,2,1,0:T(8,128)} %atm_ref.5, f32[4,40,64,256]{3,2,1,0:T(8,128)} %ocean_ref.5, s32[64,256]{1,0:T(8,128)S(1)} %copy-done.1, f32[2,32,128]{2,1,0:T(8,128)S(1)} %get-tuple-element.11.flux_ref, ...), custom_call_target="tpu_custom_call" | custom-call | flops 60000000 | bytes 22000000 | tf_op jit(solution)/shard_map/transport/pallas_call | solution.py:492
  41.0 0.0 all-to-all-done.1
  41.0 1.9 %sea_forcing.1 = f32[2,40,64,256]{3,2,1,0:T(8,128)} custom-call(f32[128,128]{1,0:T(8,128)S(1)} %bitcast.6, s32[64,256]{1,0:T(8,128)S(1)} %copy-done.1, f32[2,40,64,256]{3,2,1,0:T(8,128)} %get-tuple-element.19.before_ref), custom_call_target="tpu_custom_call", output_to_operand_aliasing={{}: (2, {})} | custom-call | flops 4000000 | bytes 600000 | tf_op jit(solution)/shard_map/sea_forcing/pallas_call | solution.py:188
Async XLA Ops:
  3.4 18.0 %all-to-all-start = ((f32[16,8,128]{2,1,0:T(8,128)}), f32[16,8,128]{2,1,0:T(8,128)S(1)}, u32[]{:S(2)}, u32[]{:S(2)}) async-start(f32[16,8,128]{2,1,0:T(8,128)} %sea_send.1), calls=%async_computation | async-start | bytes 131072 | tf_op jit(solution)/shard_map/all_to_all | solution.py:535
  10.8 10.6 %copy-start = (f32[24,128,128]{2,1,0:T(8,128)S(1)}, f32[24,128,128]{2,1,0:T(8,128)}, u32[]{:S(2)}) copy-start(f32[24,128,128]{2,1,0:T(8,128)} %weights_ref.3) | copy-start | bytes 4718596
  16.1 14.8 %copy-start.1 = (s32[64,256]{1,0:T(8,128)S(1)}, s32[64,256]{1,0:T(8,128)}, u32[]{:S(2)}) copy-start(s32[64,256]{1,0:T(8,128)} %land_ref.3) | copy-start | bytes 196612
  16.1 14.7 %collective-permute-start = (f32[432,128]{1,0:T(8,128)S(1)}, f32[432,128]{1,0:T(8,128)S(1)}, u32[]{:S(2)}, u32[]{:S(2)}) collective-permute-start(f32[432,128]{1,0:T(8,128)S(1)} %get-tuple-element.12), channel_id=1, source_target_pairs={{0,2},{2,4},{4,6},{6,8},{8,10},{10,12},{12,14},{1,3},{3,5},{5,7},{... | collective-permute-start | bytes 663560 | tf_op jit(solution)/shard_map/ppermute | solution.py:538
  20.1 10.8 %collective-permute-start.1 = (f32[432,128]{1,0:T(8,128)S(1)}, f32[432,128]{1,0:T(8,128)S(1)}, u32[]{:S(2)}, u32[]{:S(2)}) collective-permute-start(f32[432,128]{1,0:T(8,128)S(1)} %get-tuple-element.13), channel_id=1, source_target_pairs={{2,0},{4,2},{6,4},{8,6},{10,8},{12,10},{14,12},{3,1},{5,3},{7,5},{... | collective-permute-start | bytes 663560 | tf_op jit(solution)/shard_map/ppermute | solution.py:539
  21.4 2.6 %collective-permute-start.2 = (f32[128,128]{1,0:T(8,128)S(1)}, f32[128,128]{1,0:T(8,128)S(1)}, u32[]{:S(2)}, u32[]{:S(2)}) collective-permute-start(f32[128,128]{1,0:T(8,128)S(1)} %get-tuple-element.14.mine_ref), channel_id=1, source_target_pairs={{0,1},{1,0},{2,3},{3,2},{4,5},{5,4},{6,7},{7,6},{8,9},{9,8},{10,11... | collective-permute-start | bytes 196616 | tf_op jit(solution)/shard_map/ppermute | solution.py:537
  24.0 17.0 %all-to-all-start.1 = ((f32[16,8,128]{2,1,0:T(8,128)}), f32[16,8,128]{2,1,0:T(8,128)S(1)}, u32[]{:S(2)}, u32[]{:S(2)}) async-start(f32[16,8,128]{2,1,0:T(8,128)} %get-tuple-element.18), calls=%async_computation.1 | async-start | bytes 131072 | tf_op jit(solution)/shard_map/all_to_all | solution.py:542

commit v3 on v2

v3 whole, which is shorter than its diff:
```python
import functools

import jax
import jax.numpy as jnp
from jax import lax
from jax.experimental import pallas as pl
from jax.experimental.pallas import tpu as pltpu
from jax.sharding import PartitionSpec as P

WIN = 128
CAP = 2
ROWS = 4
LANES = 128
SUB = 8

time_step = 0.1
diffusion = 0.2
VMEM_LIMIT = 40 * 1024 * 1024


def held(array):
    return pltpu.with_memory_space_constraint(array, pltpu.VMEM)


def left(array):
    return pltpu.with_memory_space_constraint(array, pltpu.HBM)


def lane_of(shape):
    return lax.broadcasted_iota(jnp.int32, shape, len(shape) - 1)


def row_of(shape):
    return lax.broadcasted_iota(jnp.int32, shape, len(shape) - 2)


def send_blocks(pick, count, weights_ref, dest_ref, window_ref, picked_ref, counts_ref, out_ref):
    blocks = weights_ref.shape[0]
    out_ref[...] = jnp.zeros_like(out_ref)

    def clear(d, carry):
        counts_ref[d] = 0
        return carry

    lax.fori_loop(0, out_ref.shape[0], clear, 0)
    picked_ref[...] = jnp.zeros_like(picked_ref)
    for k in range(blocks):
        for f in range(count):
            picked_ref[k, pl.ds(f, 1), :] = pick(k, f)
    row = row_of((SUB, LANES))
    lane = lane_of((SUB, LANES))
    for k in range(blocks):
        values = picked_ref[k]
        high = values.astype(jnp.bfloat16)
        low = (values - high.astype(jnp.float32)).astype(jnp.bfloat16)
        left = jnp.concatenate([high.astype(jnp.float32), low.astype(jnp.float32)], axis=0).astype(jnp.bfloat16)
        weight = weights_ref[k]
        weight_high = weight.astype(jnp.bfloat16)
        weight_low = (weight - weight_high.astype(jnp.float32)).astype(jnp.bfloat16)
        right = jnp.concatenate([weight_high, weight_low], axis=0)
        product = lax.dot_general(left, right, (((1,), (1,)), ((), ())), preferred_element_type=jnp.float32)
        total = product[:SUB, :WIN] + (product[SUB:, :WIN] + product[:SUB, WIN:])
        d = dest_ref[k]
        slot = counts_ref[d]
        counts_ref[d] = slot + 1
        onehot = jnp.where(lane == window_ref[k], 1.0, 0.0)
        total = jnp.where(row == ROWS - 1, onehot, jnp.where(row < count, total, 0.0))
        total = jnp.where(slot == 0, total, jnp.concatenate([total[ROWS:], total[:ROWS]], axis=0))
        out_ref[d] = out_ref[d] + total


def receive_blocks(arrived_ref, count):
    slots = arrived_ref.shape[0] // ROWS
    onehot = arrived_ref[pl.ds(ROWS - 1, slots, stride=ROWS), :]
    fields = [arrived_ref[pl.ds(f, slots, stride=ROWS), :] for f in range(count)]
    return [
        lax.dot_general(
            onehot, field, (((0,), (0,)), ((), ())), precision=lax.Precision.HIGHEST, preferred_element_type=jnp.float32
        )
        for field in fields
    ]


def index_copies(refs, held_refs, sems):
    return [pltpu.make_async_copy(src, dst, sems.at[i]) for i, (src, dst) in enumerate(zip(refs, held_refs))]


def air_send_kernel(
    dest_hbm,
    source_hbm,
    window_hbm,
    arrived_ref,
    some_air_ref,
    weights_ref,
    out_ref,
    flux_ref,
    picked_ref,
    counts_ref,
    dest_ref,
    source_ref,
    window_ref,
    sems,
):
    indices = index_copies((dest_hbm, source_hbm, window_hbm), (dest_ref, source_ref, window_ref), sems)
    for copy in indices:
        copy.start()
    rows = some_air_ref.shape[2]
    surface = [some_air_ref[f, 0] for f in range(4)]
    on_air = [field[:rows] for field in receive_blocks(arrived_ref, 3)]
    relative_u = surface[2] - on_air[1]
    relative_v = surface[3] - on_air[2]
    wind_speed = jnp.sqrt(relative_u * relative_u + relative_v * relative_v + 1.0)
    flux_ref[0] = 0.5 * wind_speed * (on_air[0] - surface[0])
    flux_ref[1] = 0.4 * wind_speed * (0.8 * on_air[0] - surface[1])

    for copy in indices:
        copy.wait()

    def pick(k, f):
        return flux_ref[f, pl.ds(source_ref[k], 1), :]

    send_blocks(pick, 2, weights_ref, dest_ref, window_ref, picked_ref, counts_ref, out_ref)


def air_send(arrived, some_air, weights, dest, source, window):
    blocks = weights.shape[0]
    tiles = arrived.shape[0]
    vmem = pl.BlockSpec(memory_space=pltpu.VMEM)
    hbm = pl.BlockSpec(memory_space=pltpu.HBM)
    return pl.pallas_call(
        air_send_kernel,
        in_specs=[hbm] * 3 + [vmem] * 3,
        out_specs=(vmem, vmem),
        out_shape=(
            pltpu.VMEM((tiles, CAP * ROWS, WIN), jnp.float32),
            pltpu.VMEM((2,) + some_air.shape[2:], jnp.float32),
        ),
        scratch_shapes=[pltpu.VMEM((blocks, SUB, WIN), jnp.float32), pltpu.SMEM((tiles,), jnp.int32)]
        + [pltpu.SMEM((blocks,), jnp.int32)] * 3
        + [pltpu.SemaphoreType.DMA((3,))],
        compiler_params=pltpu.CompilerParams(vmem_limit_bytes=VMEM_LIMIT),
        cost_estimate=pl.CostEstimate(flops=blocks * 2 * 16 * 128 * 256, bytes_accessed=2000000, transcendentals=0),
        name="air_send",
    )(
        left(dest),
        left(source),
        left(window),
        held(arrived.reshape(tiles * CAP * ROWS, WIN)),
        some_air,
        held(weights),
    )


def sea_forcing_kernel(arrived_ref, land_ref, top_ref, before_ref, after_ref, summed_ref, new_ref, sem):
    del before_ref
    rows, cols = land_ref.shape
    halves = cols // WIN
    for f, field in enumerate(receive_blocks(arrived_ref, 2)):
        summed_ref[f] = field
        for h in range(halves):
            span = pl.ds(h * WIN, WIN)
            forcing = summed_ref[f, pl.ds(h, rows, stride=halves), :] * (-0.5, 0.3)[f]
            change = jnp.where(land_ref[:, span] == 1, time_step * forcing, 0.0)
            new_ref[f, :, span] = top_ref[f, :, span] + change
    copy = pltpu.make_async_copy(new_ref, after_ref.at[:, 0], sem)
    copy.start()
    copy.wait()


def add_sea_forcing(arrived, land, top, sea_next):
    tiles = arrived.shape[0]
    rows, cols = land.shape
    vmem = pl.BlockSpec(memory_space=pltpu.VMEM)
    hbm = pl.BlockSpec(memory_space=pltpu.HBM)
    return pl.pallas_call(
        sea_forcing_kernel,
        in_specs=[vmem, vmem, vmem, hbm],
        out_specs=hbm,
        out_shape=jax.ShapeDtypeStruct(sea_next.shape, jnp.float32),
        scratch_shapes=[
            pltpu.VMEM((2, rows * cols // WIN, WIN), jnp.float32),
            pltpu.VMEM((2, rows, cols), jnp.float32),
            pltpu.SemaphoreType.DMA(()),
        ],
        input_output_aliases={3: 0},
        compiler_params=pltpu.CompilerParams(vmem_limit_bytes=VMEM_LIMIT),
        cost_estimate=pl.CostEstimate(flops=4000000, bytes_accessed=600000, transcendentals=0),
        name="sea_forcing",
    )(held(arrived.reshape(tiles * CAP * ROWS, WIN)), held(land), top, sea_next)


def padded_levels(levels):
    return -(-levels // SUB) * SUB


CHUNKS = 4


def first_kernel(
    dest_hbm,
    source_hbm,
    window_hbm,
    atm_ref,
    ocean_ref,
    weights_ref,
    out_ref,
    first_ref,
    second_ref,
    y_ref,
    some_air_ref,
    air,
    sea,
    sea_v,
    low,
    high,
    weights,
    top,
    windows,
    picked,
    counts,
    dest_ref,
    source_ref,
    window_ref,
    sems,
    weight_sems,
    top_sems,
    index_sems,
):
    air_levels, air_rows = atm_ref.shape[1:3]
    sea_levels, sea_rows, sea_cols = ocean_ref.shape[1:]
    halves = sea_cols // WIN
    pitch = padded_levels(air_levels)
    gx, gy, last_gx = lax.axis_index("gx"), lax.axis_index("gy"), lax.axis_size("gx") - 1
    even = gx % 2 == 0
    at_end = (gx == 0) | (gx == last_gx)
    edge = jnp.where(gy == 0, LANES - 1, 0)
    span = pl.ds(pl.multiple_of(jnp.where(gy == 0, sea_cols - LANES, 0), LANES), LANES)
    a, o = air_levels // CHUNKS, sea_levels // CHUNKS

    tops = [pltpu.make_async_copy(ocean_ref.at[f, 0], top.at[i], top_sems.at[i]) for i, f in enumerate((0, 2, 3))]
    weights_in = pltpu.make_async_copy(weights_ref, weights, weight_sems)

    def copies(chunk):
        air_span, sea_span = pl.ds(chunk * a, a), pl.ds(chunk * o, o)
        pairs = [
            (atm_ref.at[:, air_span], air.at[:, air_span]),
            (ocean_ref.at[pl.ds(0, 2), sea_span, :, span], sea.at[:, sea_span]),
            (ocean_ref.at[3, sea_span, :, span], sea_v.at[sea_span]),
            (ocean_ref.at[pl.ds(0, 3), sea_span, pl.ds(0, SUB)], low.at[:, sea_span]),
            (ocean_ref.at[pl.ds(0, 3), sea_span, pl.ds(sea_rows - SUB, SUB)], high.at[:, sea_span]),
        ]
        return [pltpu.make_async_copy(src, dst, sems.at[chunk, i]) for i, (src, dst) in enumerate(pairs)]

    indices = index_copies((dest_hbm, source_hbm, window_hbm), (dest_ref, source_ref, window_ref), index_sems)
    for copy in indices + tops:
        copy.start()
    weights_in.start()
    for chunk in range(CHUNKS):
        for copy in copies(chunk):
            copy.start()

    for copy in indices + tops:
        copy.wait()
    for f in range(3):
        for h in range(halves):
            windows[f, pl.ds(h, sea_rows, stride=halves), :] = top[f, :, pl.ds(h * WIN, WIN)]
    weights_in.wait()

    def pick(k, f):
        return windows[f, pl.ds(source_ref[k], 1), :]

    send_blocks(pick, 3, weights, dest_ref, window_ref, picked, counts, out_ref)

    for f in range(3):
        for ref in (first_ref, second_ref):
            ref[pl.ds((f + 1) * pitch - SUB, SUB), :] = jnp.zeros((SUB, LANES), jnp.float32)

    def put_rows(to, low_row, high_row):
        first_ref[pl.ds(to, 1), :] = jnp.where(even, high_row, low_row)
        second_ref[pl.ds(to, 1), :] = jnp.where(at_end, 0.0, jnp.where(even, low_row, high_row))

    def put(total, column, to, lane):
        return jnp.where(lane == to, pltpu.roll(column, (to - edge + LANES) % LANES, 1), total)

    air_lane, sea_lane = lane_of((air_rows, LANES)), lane_of((sea_rows, LANES))
    tracers = v = jnp.zeros((air_rows, LANES), jnp.float32)
    total = jnp.zeros((sea_rows, LANES), jnp.float32)
    for chunk in range(CHUNKS):
        for copy in copies(chunk):
            copy.wait()
        if chunk == 0:
            some_air_ref[...] = air[:, : some_air_ref.shape[1]]
        for level in range(chunk * a, (chunk + 1) * a):
            tracers = put(tracers, air[0, level], level, air_lane)
            tracers = put(tracers, air[1, level], LANES // 2 + level, air_lane)
            v = put(v, air[3, level], level, air_lane)
            for f in range(3):
                put_rows(f * pitch + level, air[f, level, pl.ds(0, 1), :], air[f, level, pl.ds(air_rows - 1, 1), :])
        for level in range(chunk * o, (chunk + 1) * o):
            total = put(total, sea[0, level], level, sea_lane)
            total = put(total, sea[1, level], sea_levels + level, sea_lane)
            total = put(total, sea_v[level], 2 * sea_levels + level, sea_lane)
            for f in range(3):
                for h in range(halves):
                    tile = pl.ds(h * WIN, WIN)
                    put_rows(
                        3 * pitch + (f * halves + h) * sea_levels + level,
                        low[f, level, pl.ds(0, 1), tile],
                        high[f, level, pl.ds(SUB - 1, 1), tile],
                    )
    y_ref[:air_rows] = tracers
    y_ref[air_rows : 2 * air_rows] = v
    y_ref[2 * air_rows :] = total


def first(tiles, atm, ocean, weights, dest, source, window):
    blocks = weights.shape[0]
    air_levels, air_rows, _ = atm.shape[1:]
    sea_levels, sea_rows, sea_cols = ocean.shape[1:]
    xrows = 3 * padded_levels(air_levels) + 3 * sea_levels * (sea_cols // WIN)
    yrows = 2 * air_rows + sea_rows
    vmem = pl.BlockSpec(memory_space=pltpu.VMEM)
    hbm = pl.BlockSpec(memory_space=pltpu.HBM)
    return pl.pallas_call(
        first_kernel,
        in_specs=[hbm] * 6,
        out_specs=[vmem] * 5,
        out_shape=(
            pltpu.VMEM((tiles, CAP * ROWS, WIN), jnp.float32),
            pltpu.VMEM((xrows, LANES), jnp.float32),
            pltpu.VMEM((xrows, LANES), jnp.float32),
            pltpu.VMEM((yrows, LANES), jnp.float32),
            pltpu.VMEM((4, air_levels // STEPS, air_rows, LANES), jnp.float32),
        ),
        scratch_shapes=[
            pltpu.VMEM(atm.shape, jnp.float32),
            pltpu.VMEM((2, sea_levels, sea_rows, LANES), jnp.float32),
            pltpu.VMEM((sea_levels, sea_rows, LANES), jnp.float32),
            pltpu.VMEM((3, sea_levels, SUB, sea_cols), jnp.float32),
            pltpu.VMEM((3, sea_levels, SUB, sea_cols), jnp.float32),
            pltpu.VMEM(weights.shape, jnp.float32),
            pltpu.VMEM((3, sea_rows, sea_cols), jnp.float32),
            pltpu.VMEM((3, sea_rows * sea_cols // WIN, WIN), jnp.float32),
            pltpu.VMEM((blocks, SUB, WIN), jnp.float32),
            pltpu.SMEM((tiles,), jnp.int32),
            pltpu.SMEM((blocks,), jnp.int32),
            pltpu.SMEM((blocks,), jnp.int32),
            pltpu.SMEM((blocks,), jnp.int32),
            pltpu.SemaphoreType.DMA((CHUNKS, 5)),
            pltpu.SemaphoreType.DMA(()),
            pltpu.SemaphoreType.DMA((3,)),
            pltpu.SemaphoreType.DMA((3,)),
        ],
        compiler_params=pltpu.CompilerParams(vmem_limit_bytes=VMEM_LIMIT),
        cost_estimate=pl.CostEstimate(flops=30000000, bytes_accessed=12000000, transcendentals=0),
        name="first",
    )(left(dest), left(source), left(window), left(atm), left(ocean), left(weights))


STEPS = 5
PAD = 8
SHIFTED = (3,)


def beyond_columns(gy, mine, v_mine, other, v_other):
    scale, mixing = 0.25 * time_step, time_step * diffusion
    sign = jnp.where(gy == 0, -scale, scale)
    return mixing * other + sign * ((v_mine + v_other) * other + v_other * mine)


def shift_matrix():
    shape = (2 * LANES, 2 * LANES)
    source, to = row_of(shape) % LANES, lane_of(shape)
    left = jnp.where(to < LANES, (to + 1) % LANES, (to + LANES - 1) % LANES)
    return jnp.where(source == left, 1.0, 0.0).astype(jnp.bfloat16)


def shifted_rows(rows, matrix):
    high = rows.astype(jnp.bfloat16)
    low = (rows - high.astype(jnp.float32)).astype(jnp.bfloat16)
    return jnp.dot(jnp.concatenate([high, low], axis=1), matrix, preferred_element_type=jnp.float32)


def step_level(ref, index, shifted, groups, halves, beyond, write):
    lane = lane_of((SUB, LANES))
    first_lane, last_lane = lane == 0, lane == LANES - 1
    scale, mixing = 0.25 * time_step, time_step * diffusion

    def rows(f, h, r, offset):
        return ref[index(f, h) + (pl.ds(PAD + r * SUB + offset, SUB), slice(None))]

    def along_y(f, r, tiles):
        if f in SHIFTED:
            left, right = zip(*[shifted(f, r, h) for h in range(halves)])
            left, right = list(left), list(right)
        else:
            right = [pltpu.roll(t, 1, 1) for t in tiles]
            left = [pltpu.roll(t, LANES - 1, 1) for t in tiles]
        lows = [jnp.where(first_lane, b, t) for b, t in zip([0.0] + right[:-1], right)]
        highs = [jnp.where(last_lane, b, t) for b, t in zip(left[1:] + [0.0], left)]
        return lows, highs

    for r in range(groups):
        q = [[rows(f, h, r, 0) for h in range(halves)] for f in range(2)]
        v = [scale * rows(3, h, r, 0) for h in range(halves)]
        v_low, v_high = along_y(3, r, v)
        sides = [along_y(f, r, q[f]) for f in range(2)]
        for h in range(halves):
            u, u_low, u_high = (scale * rows(2, h, r, offset) for offset in (0, -1, 1))
            centre = (1.0 - 4.0 * mixing) + ((u_low - u_high) + (v_low[h] - v_high[h]))
            x_high, x_low = (mixing - u) - u_high, (mixing + u) + u_low
            y_high, y_low = (mixing - v[h]) - v_high[h], (mixing + v[h]) + v_low[h]
            for f in range(2):
                new = centre * q[f][h] + (x_high * rows(f, h, r, 1) + x_low * rows(f, h, r, -1))
                new = new + (y_high * sides[f][1][h] + y_low * sides[f][0][h])
                write(f, r, h, new + beyond(f, r, h), q[f][h])


def transport_kernel(
    atm_ref,
    ocean_ref,
    some_air_ref,
    land_ref,
    flux_ref,
    first_ref,
    second_ref,
    mine_ref,
    y_ref,
    air_ref,
    sea_ref,
    top_ref,
    air,
    sea,
    air_new,
    sea_new,
    air_edge,
    sea_edge,
    air_shifted,
    sea_shifted,
    matrix,
    in_sems,
    out_sems,
):
    all_air, air_rows = atm_ref.shape[1:3]
    all_sea, sea_rows, sea_cols = ocean_ref.shape[1:]
    a, o = all_air // STEPS, all_sea // STEPS
    halves = sea_cols // LANES
    pitch = padded_levels(all_air)
    even, gy = lax.axis_index("gx") % 2 == 0, lax.axis_index("gy")

    def air_in(step):
        levels = pl.ds(step * a, a)
        yield pltpu.make_async_copy(
            atm_ref.at[:, levels], air.at[:, levels, pl.ds(PAD, air_rows)], in_sems.at[step, halves]
        )

    def sea_in(step):
        levels = pl.ds(step * o, o)
        for h in range(halves):
            yield pltpu.make_async_copy(
                ocean_ref.at[:, levels, :, pl.ds(h * LANES, LANES)],
                sea.at[h, :, levels, pl.ds(PAD, sea_rows)],
                in_sems.at[step, h],
            )

    def air_out(step):
        levels = pl.ds(step * a, a)
        return pltpu.make_async_copy(air_new.at[:, levels], air_ref.at[:, levels], out_sems.at[step, 0])

    def sea_out(step):
        levels = pl.ds(step * o, o)
        return pltpu.make_async_copy(sea_new.at[:, levels], sea_ref.at[:, levels], out_sems.at[step, 1])

    for step in range(STEPS):
        for copy in (*sea_in(step), *(air_in(step) if step > 0 else ())):
            copy.start()
    matrix[...] = shift_matrix()
    air[:, :a, pl.ds(PAD, air_rows), :] = some_air_ref[...]

    lane = lane_of((air_rows, LANES))
    mine, other = mine_ref[:air_rows], y_ref[:air_rows]

    def twice(v):
        return jnp.where(lane < LANES // 2, v, pltpu.roll(v, LANES // 2, 1))

    v_mine, v_other = twice(mine_ref[air_rows : 2 * air_rows]), twice(y_ref[air_rows : 2 * air_rows])
    air_edge[...] = beyond_columns(gy, mine, v_mine, other, v_other)
    lane = lane_of((sea_rows, LANES))
    mine, other = mine_ref[2 * air_rows :], y_ref[2 * air_rows :]

    def both(columns):
        first, second = (pltpu.roll(columns, LANES - n * all_sea, 1) for n in (2, 1))
        return jnp.where(lane < all_sea, first, second)

    sea_edge[...] = beyond_columns(gy, mine, both(mine), other, both(other))

    edge = jnp.where(gy == 0, LANES - 1, 0)
    lane = lane_of((SUB, LANES))
    at_first, at_last = (lane == 0) & (gy != 0), (lane == LANES - 1) & (gy == 0)
    at_edge = lane == edge

    def column(ref, r, at):
        return pltpu.roll(ref[pl.ds(r * SUB, SUB), :], (edge - at + LANES) % LANES, 1)

    def x_rows(at):
        one, other = first_ref[pl.ds(at, 1), :], second_ref[pl.ds(at, 1), :]
        return jnp.where(even, other, one), jnp.where(even, one, other)

    def some_air(step):
        for j in range(a):
            level = step * a + j
            for f in range(3):
                before, after = x_rows(f * pitch + level)
                air[f, level, pl.ds(PAD - 1, 1), :] = before
                air[f, level, pl.ds(PAD + air_rows, 1), :] = after
        for i, f in enumerate(SHIFTED):
            rows = air[f, pl.ds(step * a, a), pl.ds(PAD, air_rows), :].reshape(a * air_rows, LANES)
            air_shifted[i] = shifted_rows((0.25 * time_step if f == 3 else 1.0) * rows, matrix[...])
        stores = []
        for j in range(a):
            level = step * a + j

            def beyond(f, r, h):
                return jnp.where(at_edge, column(air_edge, r, f * (LANES // 2) + level), 0.0)

            def shifted(f, r, h):
                rows = pl.ds(j * air_rows + r * SUB, SUB)
                i = SHIFTED.index(f)
                return air_shifted[i, rows, pl.ds(0, LANES)], air_shifted[i, rows, pl.ds(LANES, LANES)]

            def write(f, r, h, new, q):
                stores.append((f, level, pl.ds(r * SUB, SUB), new))

            step_level(air, lambda f, h: (f, level), shifted, air_rows // SUB, 1, beyond, write)
        for *place, new in stores:
            air_new[tuple(place)] = new

    def some_sea(step):
        for j in range(o):
            level = step * o + j
            for f in range(3):
                for h in range(halves):
                    before, after = x_rows(3 * pitch + (f * halves + h) * all_sea + level)
                    sea[h, f, level, pl.ds(PAD - 1, 1), :] = before
                    sea[h, f, level, pl.ds(PAD + sea_rows, 1), :] = after
        for i, f in enumerate(SHIFTED):
            for h in range(halves):
                rows = sea[h, f, pl.ds(step * o, o), pl.ds(PAD, sea_rows), :].reshape(o * sea_rows, LANES)
                sea_shifted[i, h] = shifted_rows((0.25 * time_step if f == 3 else 1.0) * rows, matrix[...])
        stores = []
        for j in range(o):
            level = step * o + j
            columns = {}

            def beyond(f, r, h):
                if (f, r) not in columns:
                    columns[f, r] = column(sea_edge, r, f * all_sea + level)
                added = columns[f, r]
                if h == 0:
                    return jnp.where(at_first, added, 0.0)
                return jnp.where(at_last, added, 0.0) if h == halves - 1 else 0.0

            def shifted(f, r, h):
                rows = pl.ds(j * sea_rows + r * SUB, SUB)
                i = SHIFTED.index(f)
                return sea_shifted[i, h, rows, pl.ds(0, LANES)], sea_shifted[i, h, rows, pl.ds(LANES, LANES)]

            def write(f, r, h, new, q):
                rows, span = pl.ds(r * SUB, SUB), pl.ds(h * LANES, LANES)
                stores.append((f, level, rows, span, jnp.where(land_ref[rows, span] == 1, new, q)))

            step_level(sea, lambda f, h: (h, f, level), shifted, sea_rows // SUB, halves, beyond, write)
        for *place, new in stores:
            sea_new[tuple(place)] = new

    some_air(0)
    for f in range(2):
        air_new[f, 0] = air_new[f, 0] + time_step * flux_ref[f]
    air_out(0).start()

    def some_levels(step, carry):
        for copy in sea_in(step):
            copy.wait()
        some_sea(step)
        sea_out(step).start()

        @pl.when(step == 0)
        def _():
            top_ref[...] = sea_new[:, 0]

        @pl.when(step > 0)
        def _():
            for copy in air_in(step):
                copy.wait()
            some_air(step)
            air_out(step).start()

        return carry

    lax.fori_loop(0, STEPS, some_levels, 0)
    for step in range(STEPS):
        air_out(step).wait()
        sea_out(step).wait()


def transport(atm, ocean, some_air, land, flux, first_rows, second_rows, mine, y):
    air_levels, air_rows, _ = atm.shape[1:]
    sea_levels, sea_rows, sea_cols = ocean.shape[1:]
    halves = sea_cols // LANES
    vmem = pl.BlockSpec(memory_space=pltpu.VMEM)
    hbm = pl.BlockSpec(memory_space=pltpu.HBM)
    air_shape, sea_shape = (2,) + atm.shape[1:], (2,) + ocean.shape[1:]
    return pl.pallas_call(
        transport_kernel,
        in_specs=[hbm, hbm] + [vmem] * 7,
        out_specs=[hbm, hbm, vmem],
        out_shape=(
            jax.ShapeDtypeStruct(air_shape, jnp.float32),
            jax.ShapeDtypeStruct(sea_shape, jnp.float32),
            pltpu.VMEM((2, sea_rows, sea_cols), jnp.float32),
        ),
        scratch_shapes=[
            pltpu.VMEM((4, air_levels, air_rows + 2 * PAD, LANES), jnp.float32),
            pltpu.VMEM((halves, 4, sea_levels, sea_rows + 2 * PAD, LANES), jnp.float32),
            pltpu.VMEM(air_shape, jnp.float32),
            pltpu.VMEM(sea_shape, jnp.float32),
            pltpu.VMEM((air_rows, LANES), jnp.float32),
            pltpu.VMEM((sea_rows, LANES), jnp.float32),
            pltpu.VMEM((len(SHIFTED), air_levels // STEPS * air_rows, 2 * LANES), jnp.float32),
            pltpu.VMEM((len(SHIFTED), halves, sea_levels // STEPS * sea_rows, 2 * LANES), jnp.float32),
            pltpu.VMEM((2 * LANES, 2 * LANES), jnp.bfloat16),
            pltpu.SemaphoreType.DMA((STEPS, halves + 1)),
            pltpu.SemaphoreType.DMA((STEPS, 2)),
        ],
        compiler_params=pltpu.CompilerParams(vmem_limit_bytes=VMEM_LIMIT),
        cost_estimate=pl.CostEstimate(flops=60000000, bytes_accessed=22000000, transcendentals=0),
        name="transport",
    )(left(atm), left(ocean), some_air, held(land), flux, held(first_rows), held(second_rows), mine, held(y))


def body(
    atm_fields,
    ocean_fields,
    land_sea,
    sea_weights,
    sea_dest,
    sea_source,
    sea_window,
    air_weights,
    air_dest,
    air_source,
    air_window,
):
    width_x, width_y = lax.axis_size("gx"), lax.axis_size("gy")
    assert width_y == 2 and width_x % 2 == 0
    tiles = width_x * width_y
    exchange = functools.partial(lax.all_to_all, axis_name=("gx", "gy"), split_axis=0, concat_axis=0, tiled=True)
    pairs = [(i, i ^ 1) for i in range(width_x)]
    other_pairs = [(i, (i + 1 if i % 2 else i - 1) % width_x) for i in range(width_x)]

    to_air, rows, other_rows, mine, some_air = first(
        tiles, atm_fields, ocean_fields, sea_weights, sea_dest.reshape(-1), sea_source, sea_window
    )
    on_air = exchange(to_air)
    side = lax.ppermute(mine, "gy", [(0, 1), (1, 0)])
    rows = lax.ppermute(rows, "gx", pairs)
    other_rows = lax.ppermute(other_rows, "gx", other_pairs)
    to_sea, fluxes = air_send(on_air, some_air, air_weights, air_dest.reshape(-1), air_source, air_window)
    to_sea, side = lax.optimization_barrier((to_sea, side))
    on_sea = exchange(to_sea)
    air_next, sea_next, top = transport(
        atm_fields, ocean_fields, some_air, land_sea, fluxes, rows, other_rows, mine, side
    )
    sea_next = add_sea_forcing(on_sea, land_sea, top, sea_next)
    return (air_next, sea_next)


def solution(mesh):
    placed = (
        P("ens", None, "gx", "gy"),
        P("ens", None, "gx", "gy"),
        P(("ens", "gx"), "gy"),
        P(("ens", "gx", "gy"), None, None),
        P(("ens", "gx", "gy"), None),
        P(("ens", "gx", "gy")),
        P(("ens", "gx", "gy")),
        P(("ens", "gx", "gy"), None, None),
        P(("ens", "gx", "gy"), None),
        P(("ens", "gx", "gy")),
        P(("ens", "gx", "gy")),
    )
    return jax.shard_map(
        body,
        mesh=mesh,
        in_specs=placed,
        out_specs=(P("ens", None, "gx", "gy"), P("ens", None, "gx", "gy")),
        check_vma=False,
    )
```

time: 43.3 us -> 38.3 us (0.88)
  Pallas kernels: 22.6 us -> 18.8 us
  starting transfers between devices: 19.5 us -> 16.1 us
  waiting for transfers between devices: 0.01 us -> 2.44 us
    pallas_call x5 -> x4, Pallas kernels: 22.6 us -> 18.8 us  [the longest x1 10 us: transport(): pl.pallas_call(transport_kernel, in_specs=[hbm, hbm] + [vmem] * 7, out_sp...]
    all_to_all x1, starting transfers between devices: 6.81 us -> 3.5 us  [body(): on_sea = exchange(to_sea)]
    all_to_all x1, waiting for transfers between devices: 0.01 us -> 1.7 us  [body(): on_air = exchange(to_air)]
    ppermute x2, waiting for transfers between devices: 0.01 us -> 0.73 us  [the longest x1 0.73 us: body(): rows = lax.ppermute(rows, 'gx', pairs)]
  transfers between devices with their start and end apart: 5 -> 5, of which waited for: 0 -> 2; matrix products, arithmetic and copies ran while one was open for 0% -> 0% of each run, Pallas kernels for 42% -> 32%
where the time goes in v3:
time: 38.3 us; the launch traced here: 38.1 us
  Pallas kernels  18.8 us (49%)
  starting transfers between devices  16.1 us (42%)
  waiting for transfers between devices  2.44 us (6%)
  between operations  0.71 us (2%)
    pallas_call x1, Pallas kernels, transport(): pl.pallas_call(transport_kernel, in_specs=[hbm, hbm] + [vmem] * 7, out_sp...  10 us
    all_to_all x1, starting transfers between devices, body(): on_air = exchange(to_air)  7.4 us
    pallas_call x1, Pallas kernels, first(): pl.pallas_call(first_kernel, in_specs=[hbm] * 6, out_specs=[vmem] * 5, ou...  5.64 us
    all_to_all x1, starting transfers between devices, body(): on_sea = exchange(to_sea)  3.5 us
    ppermute x1, starting transfers between devices, body(): other_rows = lax.ppermute(other_rows, 'gx', other_pairs)  3.27 us
    pallas_call x1, Pallas kernels, air_send(): pl.pallas_call(air_send_kernel, in_specs=[hbm] * 3 + [vmem] * 3, out_spec...  2.16 us
    ppermute x1, starting transfers between devices, body(): rows = lax.ppermute(rows, 'gx', pairs)  1.93 us
    all_to_all x1, waiting for transfers between devices, body(): on_air = exchange(to_air)  1.7 us
  transfers between devices with their start and end apart: 5, of which 2 were waited for; matrix products, arithmetic and copies ran while one was open for 0% of the time, Pallas kernels for 32%

profile of v3, /device:TPU:0, one launch (start us, length us, event | category | flops | bytes accessed | tf_op | source)
XLA Modules:
  0.0 38.1 jit_solution(9477435012223903518)
XLA Ops:
  0.6 0.0 copy-start
  0.6 0.0 copy-start.1
  0.7 5.6 %first.1 = (f32[16,8,128]{2,1,0:T(8,128)}, f32[432,128]{1,0:T(8,128)S(1)}, f32[432,128]{1,0:T(8,128)S(1)}, f32[128,128]{1,0:T(8,128)S(1)}, f32[4,12,32,128]{3,2,1,0:T(8,128)S(1)}) custom-call(s32[24]{0:T(128)} %bitcast.6, s32[24]{0:T(128)} %source_hbm.2, s32[24]{0:T(128)} %window_hbm.2, f32[4,60,32,128]{3,2,1,0:T(8,128)} %atm_ref.3, ...), custom_call_target="tpu_custom_call" | custom-call | flops 30000000 | bytes 12000000 | tf_op jit(solution)/shard_map/first/pallas_call | solution.py:324
  6.3 7.4 %all-to-all-start = ((f32[16,8,128]{2,1,0:T(8,128)}), f32[16,8,128]{2,1,0:T(8,128)S(1)}, u32[]{:S(2)}, u32[]{:S(2)}) async-start(f32[16,8,128]{2,1,0:T(8,128)} %get-tuple-element.15), calls=%async_computation | async-start | bytes 131072 | tf_op jit(solution)/shard_map/all_to_all | solution.py:664
  13.7 1.9 %collective-permute-start = (f32[432,128]{1,0:T(8,128)S(1)}, f32[432,128]{1,0:T(8,128)S(1)}, u32[]{:S(2)}, u32[]{:S(2)}) collective-permute-start(f32[432,128]{1,0:T(8,128)S(1)} %get-tuple-element.17), channel_id=1, source_target_pairs={{0,2},{2,0},{4,6},{6,4},{8,10},{10,8},{12,14},{14,12},{1,3},{3,1},... | collective-permute-start | bytes 663560 | tf_op jit(solution)/shard_map/ppermute | solution.py:666
  15.6 3.3 %collective-permute-start.1 = (f32[432,128]{1,0:T(8,128)S(1)}, f32[432,128]{1,0:T(8,128)S(1)}, u32[]{:S(2)}, u32[]{:S(2)}) collective-permute-start(f32[432,128]{1,0:T(8,128)S(1)} %get-tuple-element.18), channel_id=1, source_target_pairs={{0,14},{2,4},{4,2},{6,8},{8,6},{10,12},{12,10},{14,0},{1,15},{3,5}... | collective-permute-start | bytes 663560 | tf_op jit(solution)/shard_map/ppermute | solution.py:667
  18.9 0.0 collective-permute-start.2
  18.9 1.7 %all-to-all-done = f32[16,8,128]{2,1,0:T(8,128)S(1)} async-done(((f32[16,8,128]{2,1,0:T(8,128)}), f32[16,8,128]{2,1,0:T(8,128)S(1)}, u32[]{:S(2)}, u32[]{:S(2)}) %all-to-all-start) | async-done | bytes 65568 | tf_op jit(solution)/shard_map/all_to_all | solution.py:664
  20.6 0.0 copy-done
  20.6 2.2 %air_send.1 = (f32[16,8,128]{2,1,0:T(8,128)}, f32[2,32,128]{2,1,0:T(8,128)S(1)}) custom-call(s32[24]{0:T(128)} %bitcast.7, s32[24]{0:T(128)} %source_hbm.3, s32[24]{0:T(128)} %window_hbm.3, f32[128,128]{1,0:T(8,128)S(1)} %bitcast.5, f32[4,12,32,128]{3,2,1,0:T(8,128)S(1)} %get-tuple-element.14.some_air_ref, f32[24,128,128]{2,1,0:T(8,128)S(1)} %copy-done), custom_call_target="tpu_custom_call" | custom-call | flops 25165824 | bytes 2000000 | tf_op jit(solution)/shard_map/air_send/pallas_call | solution.py:130
  22.8 0.0 collective-permute-done.2.y_ref
  22.8 3.5 %all-to-all-start.1 = ((f32[16,8,128]{2,1,0:T(8,128)}), f32[16,8,128]{2,1,0:T(8,128)S(1)}, u32[]{:S(2)}, u32[]{:S(2)}) async-start(f32[16,8,128]{2,1,0:T(8,128)} %get-tuple-element.23), calls=%async_computation.1 | async-start | bytes 131072 | tf_op jit(solution)/shard_map/all_to_all | solution.py:670
  26.3 0.7 %collective-permute-done.first_ref = f32[432,128]{1,0:T(8,128)S(1)} collective-permute-done((f32[432,128]{1,0:T(8,128)S(1)}, f32[432,128]{1,0:T(8,128)S(1)}, u32[]{:S(2)}, u32[]{:S(2)}) %collective-permute-start) | collective-permute-done | bytes 221216 | tf_op jit(solution)/shard_map/ppermute | solution.py:666
  27.0 0.0 collective-permute-done.1.second_ref
  27.0 0.0 copy-done.1
  27.0 10.0 %transport.1 = (f32[2,60,32,128]{3,2,1,0:T(8,128)}, f32[2,40,64,256]{3,2,1,0:T(8,128)}, f32[2,64,256]{2,1,0:T(8,128)S(1)}) custom-call(f32[4,60,32,128]{3,2,1,0:T(8,128)} %atm_ref.3, f32[4,40,64,256]{3,2,1,0:T(8,128)} %ocean_ref.3, f32[4,12,32,128]{3,2,1,0:T(8,128)S(1)} %get-tuple-element.14.some_air_ref, s32[64,256]{1,0:T(8,128)S(1)} %copy-done.1, ...), custom_call_target="tpu_custom_call" | custom-call | flops 60000000 | bytes 22000000 | tf_op jit(solution)/shard_map/transport/pallas_call | solution.py:613
  37.0 0.0 all-to-all-done.1
  37.1 1.0 %sea_forcing.1 = f32[2,40,64,256]{3,2,1,0:T(8,128)} custom-call(f32[128,128]{1,0:T(8,128)S(1)} %bitcast.4, s32[64,256]{1,0:T(8,128)S(1)} %copy-done.1, f32[2,64,256]{2,1,0:T(8,128)S(1)} %get-tuple-element.24.top_ref, f32[2,40,64,256]{3,2,1,0:T(8,128)} %get-tuple-element.25.before_ref), custom_call_target="tpu_custom_call", output_to_operand_aliasing={{}: (3, {})} | custom-call | flops 4000000 | bytes 600000 | tf_op jit(solution)/shard_map/sea_forcing/pallas_call | solution.py:175
Async XLA Ops:
  0.6 20.0 %copy-start = (f32[24,128,128]{2,1,0:T(8,128)S(1)}, f32[24,128,128]{2,1,0:T(8,128)}, u32[]{:S(2)}) copy-start(f32[24,128,128]{2,1,0:T(8,128)} %weights_ref.3) | copy-start | bytes 4718596
  0.6 26.4 %copy-start.1 = (s32[64,256]{1,0:T(8,128)S(1)}, s32[64,256]{1,0:T(8,128)}, u32[]{:S(2)}) copy-start(s32[64,256]{1,0:T(8,128)} %land_ref.3) | copy-start | bytes 196612
  6.3 14.3 %all-to-all-start = ((f32[16,8,128]{2,1,0:T(8,128)}), f32[16,8,128]{2,1,0:T(8,128)S(1)}, u32[]{:S(2)}, u32[]{:S(2)}) async-start(f32[16,8,128]{2,1,0:T(8,128)} %get-tuple-element.15), calls=%async_computation | async-start | bytes 131072 | tf_op jit(solution)/shard_map/all_to_all | solution.py:664
  13.7 13.3 %collective-permute-start = (f32[432,128]{1,0:T(8,128)S(1)}, f32[432,128]{1,0:T(8,128)S(1)}, u32[]{:S(2)}, u32[]{:S(2)}) collective-permute-start(f32[432,128]{1,0:T(8,128)S(1)} %get-tuple-element.17), channel_id=1, source_target_pairs={{0,2},{2,0},{4,6},{6,4},{8,10},{10,8},{12,14},{14,12},{1,3},{3,1},... | collective-permute-start | bytes 663560 | tf_op jit(solution)/shard_map/ppermute | solution.py:666
  15.6 11.4 %collective-permute-start.1 = (f32[432,128]{1,0:T(8,128)S(1)}, f32[432,128]{1,0:T(8,128)S(1)}, u32[]{:S(2)}, u32[]{:S(2)}) collective-permute-start(f32[432,128]{1,0:T(8,128)S(1)} %get-tuple-element.18), channel_id=1, source_target_pairs={{0,14},{2,4},{4,2},{6,8},{8,6},{10,12},{12,10},{14,0},{1,15},{3,5}... | collective-permute-start | bytes 663560 | tf_op jit(solution)/shard_map/ppermute | solution.py:667
  18.9 3.9 %collective-permute-start.2 = (f32[128,128]{1,0:T(8,128)S(1)}, f32[128,128]{1,0:T(8,128)S(1)}, u32[]{:S(2)}, u32[]{:S(2)}) collective-permute-start(f32[128,128]{1,0:T(8,128)S(1)} %get-tuple-element.19.mine_ref), channel_id=1, source_target_pairs={{0,1},{1,0},{2,3},{3,2},{4,5},{5,4},{6,7},{7,6},{8,9},{9,8},{10,11... | collective-permute-start | bytes 196616 | tf_op jit(solution)/shard_map/ppermute | solution.py:665
  22.8 14.3 %all-to-all-start.1 = ((f32[16,8,128]{2,1,0:T(8,128)}), f32[16,8,128]{2,1,0:T(8,128)S(1)}, u32[]{:S(2)}, u32[]{:S(2)}) async-start(f32[16,8,128]{2,1,0:T(8,128)} %get-tuple-element.23), calls=%async_computation.1 | async-start | bytes 131072 | tf_op jit(solution)/shard_map/all_to_all | solution.py:670

commit v4 on v3

--- a/solution.py
+++ b/solution.py
@@ -656,7 +656,7 @@
     tiles = width_x * width_y
     exchange = functools.partial(lax.all_to_all, axis_name=("gx", "gy"), split_axis=0, concat_axis=0, tiled=True)
     pairs = [(i, i ^ 1) for i in range(width_x)]
-    other_pairs = [(i, (i + 1 if i % 2 else i - 1) % width_x) for i in range(width_x)]
+    other_pairs = [(i, i + 1 if i % 2 else i - 1) for i in range(1, width_x - 1)]
 
     to_air, rows, other_rows, mine, some_air = first(
         tiles, atm_fields, ocean_fields, sea_weights, sea_dest.reshape(-1), sea_source, sea_window

time: 38.3 us -> 37.6 us (0.982)
  starting transfers between devices: 16.1 us -> 13.6 us
  waiting for transfers between devices: 2.44 us -> 4.23 us
    ppermute x1, starting transfers between devices: 3.27 us -> 0.66 us  [body(): other_rows = lax.ppermute(other_rows, 'gx', other_pairs)]
    all_to_all x1, waiting for transfers between devices: 1.7 us -> 4.22 us  [body(): on_air = exchange(to_air)]
    ppermute x1, waiting for transfers between devices: 0.73 us -> 0.01 us  [body(): rows = lax.ppermute(rows, 'gx', pairs)]
  transfers between devices with their start and end apart: 5 -> 5, of which waited for: 2 -> 1; matrix products, arithmetic and copies ran while one was open for 0% -> 0% of each run, Pallas kernels for 32% -> 33%
where the time goes in v4:
time: 37.6 us; the launch traced here: 37.4 us
  Pallas kernels  18.8 us (50%)
  starting transfers between devices  13.6 us (36%)
  waiting for transfers between devices  4.23 us (11%)
  between operations  0.74 us (2%)
    pallas_call x1, Pallas kernels, transport(): pl.pallas_call(transport_kernel, in_specs=[hbm, hbm] + [vmem] * 7, out_sp...  10 us
    all_to_all x1, starting transfers between devices, body(): on_air = exchange(to_air)  7.4 us
    pallas_call x1, Pallas kernels, first(): pl.pallas_call(first_kernel, in_specs=[hbm] * 6, out_specs=[vmem] * 5, ou...  5.64 us
    all_to_all x1, waiting for transfers between devices, body(): on_air = exchange(to_air)  4.22 us
    all_to_all x1, starting transfers between devices, body(): on_sea = exchange(to_sea)  3.5 us
    pallas_call x1, Pallas kernels, air_send(): pl.pallas_call(air_send_kernel, in_specs=[hbm] * 3 + [vmem] * 3, out_spec...  2.16 us
    ppermute x1, starting transfers between devices, body(): rows = lax.ppermute(rows, 'gx', pairs)  1.93 us
    pallas_call x1, Pallas kernels, add_sea_forcing(): pl.pallas_call(sea_forcing_kernel, in_specs=[vmem, vmem, vmem, hbm], out_...  1 us
  transfers between devices with their start and end apart: 5, of which 1 were waited for; matrix products, arithmetic and copies ran while one was open for 0% of the time, Pallas kernels for 33%

profile of v4, /device:TPU:0, one launch (start us, length us, event | category | flops | bytes accessed | tf_op | source)
XLA Modules:
  0.0 37.4 jit_solution(2844580086741987656)
XLA Ops:
  0.6 0.0 copy-start
  0.6 0.0 copy-start.1
  0.7 5.6 %first.1 = (f32[16,8,128]{2,1,0:T(8,128)}, f32[432,128]{1,0:T(8,128)S(1)}, f32[432,128]{1,0:T(8,128)S(1)}, f32[128,128]{1,0:T(8,128)S(1)}, f32[4,12,32,128]{3,2,1,0:T(8,128)S(1)}) custom-call(s32[24]{0:T(128)} %bitcast.6, s32[24]{0:T(128)} %source_hbm.2, s32[24]{0:T(128)} %window_hbm.2, f32[4,60,32,128]{3,2,1,0:T(8,128)} %atm_ref.3, ...), custom_call_target="tpu_custom_call" | custom-call | flops 30000000 | bytes 12000000 | tf_op jit(solution)/shard_map/first/pallas_call | solution.py:324
  6.3 7.4 %all-to-all-start = ((f32[16,8,128]{2,1,0:T(8,128)}), f32[16,8,128]{2,1,0:T(8,128)S(1)}, u32[]{:S(2)}, u32[]{:S(2)}) async-start(f32[16,8,128]{2,1,0:T(8,128)} %get-tuple-element.15), calls=%async_computation | async-start | bytes 131072 | tf_op jit(solution)/shard_map/all_to_all | solution.py:664
  13.7 1.9 %collective-permute-start = (f32[432,128]{1,0:T(8,128)S(1)}, f32[432,128]{1,0:T(8,128)S(1)}, u32[]{:S(2)}, u32[]{:S(2)}) collective-permute-start(f32[432,128]{1,0:T(8,128)S(1)} %get-tuple-element.17), channel_id=1, source_target_pairs={{0,2},{2,0},{4,6},{6,4},{8,10},{10,8},{12,14},{14,12},{1,3},{3,1},... | collective-permute-start | bytes 663560 | tf_op jit(solution)/shard_map/ppermute | solution.py:666
  15.6 0.7 %collective-permute-start.1 = (f32[432,128]{1,0:T(8,128)S(1)}, f32[432,128]{1,0:T(8,128)S(1)}, u32[]{:S(2)}, u32[]{:S(2)}) collective-permute-start(f32[432,128]{1,0:T(8,128)S(1)} %get-tuple-element.18), channel_id=1, source_target_pairs={{2,4},{4,2},{6,8},{8,6},{10,12},{12,10},{3,5},{5,3},{7,9},{9,7},{1... | collective-permute-start | bytes 663560 | tf_op jit(solution)/shard_map/ppermute | solution.py:667
  16.3 0.1 collective-permute-start.2
  16.4 4.2 %all-to-all-done = f32[16,8,128]{2,1,0:T(8,128)S(1)} async-done(((f32[16,8,128]{2,1,0:T(8,128)}), f32[16,8,128]{2,1,0:T(8,128)S(1)}, u32[]{:S(2)}, u32[]{:S(2)}) %all-to-all-start) | async-done | bytes 65568 | tf_op jit(solution)/shard_map/all_to_all | solution.py:664
  20.6 0.0 copy-done
  20.6 2.2 %air_send.1 = (f32[16,8,128]{2,1,0:T(8,128)}, f32[2,32,128]{2,1,0:T(8,128)S(1)}) custom-call(s32[24]{0:T(128)} %bitcast.7, s32[24]{0:T(128)} %source_hbm.3, s32[24]{0:T(128)} %window_hbm.3, f32[128,128]{1,0:T(8,128)S(1)} %bitcast.5, f32[4,12,32,128]{3,2,1,0:T(8,128)S(1)} %get-tuple-element.14.some_air_ref, f32[24,128,128]{2,1,0:T(8,128)S(1)} %copy-done), custom_call_target="tpu_custom_call" | custom-call | flops 25165824 | bytes 2000000 | tf_op jit(solution)/shard_map/air_send/pallas_call | solution.py:130
  22.8 0.0 collective-permute-done.2.y_ref
  22.8 3.5 %all-to-all-start.1 = ((f32[16,8,128]{2,1,0:T(8,128)}), f32[16,8,128]{2,1,0:T(8,128)S(1)}, u32[]{:S(2)}, u32[]{:S(2)}) async-start(f32[16,8,128]{2,1,0:T(8,128)} %get-tuple-element.23), calls=%async_computation.1 | async-start | bytes 131072 | tf_op jit(solution)/shard_map/all_to_all | solution.py:670
  26.3 0.0 collective-permute-done.first_ref
  26.3 0.0 collective-permute-done.1.second_ref
  26.3 0.0 copy-done.1
  26.3 10.0 %transport.1 = (f32[2,60,32,128]{3,2,1,0:T(8,128)}, f32[2,40,64,256]{3,2,1,0:T(8,128)}, f32[2,64,256]{2,1,0:T(8,128)S(1)}) custom-call(f32[4,60,32,128]{3,2,1,0:T(8,128)} %atm_ref.3, f32[4,40,64,256]{3,2,1,0:T(8,128)} %ocean_ref.3, f32[4,12,32,128]{3,2,1,0:T(8,128)S(1)} %get-tuple-element.14.some_air_ref, s32[64,256]{1,0:T(8,128)S(1)} %copy-done.1, ...), custom_call_target="tpu_custom_call" | custom-call | flops 60000000 | bytes 22000000 | tf_op jit(solution)/shard_map/transport/pallas_call | solution.py:613
  36.4 0.0 all-to-all-done.1
  36.4 1.0 %sea_forcing.1 = f32[2,40,64,256]{3,2,1,0:T(8,128)} custom-call(f32[128,128]{1,0:T(8,128)S(1)} %bitcast.4, s32[64,256]{1,0:T(8,128)S(1)} %copy-done.1, f32[2,64,256]{2,1,0:T(8,128)S(1)} %get-tuple-element.24.top_ref, f32[2,40,64,256]{3,2,1,0:T(8,128)} %get-tuple-element.25.before_ref), custom_call_target="tpu_custom_call", output_to_operand_aliasing={{}: (3, {})} | custom-call | flops 4000000 | bytes 600000 | tf_op jit(solution)/shard_map/sea_forcing/pallas_call | solution.py:175
Async XLA Ops:
  0.6 20.0 %copy-start = (f32[24,128,128]{2,1,0:T(8,128)S(1)}, f32[24,128,128]{2,1,0:T(8,128)}, u32[]{:S(2)}) copy-start(f32[24,128,128]{2,1,0:T(8,128)} %weights_ref.3) | copy-start | bytes 4718596
  0.6 25.7 %copy-start.1 = (s32[64,256]{1,0:T(8,128)S(1)}, s32[64,256]{1,0:T(8,128)}, u32[]{:S(2)}) copy-start(s32[64,256]{1,0:T(8,128)} %land_ref.3) | copy-start | bytes 196612
  6.3 14.3 %all-to-all-start = ((f32[16,8,128]{2,1,0:T(8,128)}), f32[16,8,128]{2,1,0:T(8,128)S(1)}, u32[]{:S(2)}, u32[]{:S(2)}) async-start(f32[16,8,128]{2,1,0:T(8,128)} %get-tuple-element.15), calls=%async_computation | async-start | bytes 131072 | tf_op jit(solution)/shard_map/all_to_all | solution.py:664
  13.7 12.6 %collective-permute-start = (f32[432,128]{1,0:T(8,128)S(1)}, f32[432,128]{1,0:T(8,128)S(1)}, u32[]{:S(2)}, u32[]{:S(2)}) collective-permute-start(f32[432,128]{1,0:T(8,128)S(1)} %get-tuple-element.17), channel_id=1, source_target_pairs={{0,2},{2,0},{4,6},{6,4},{8,10},{10,8},{12,14},{14,12},{1,3},{3,1},... | collective-permute-start | bytes 663560 | tf_op jit(solution)/shard_map/ppermute | solution.py:666
  15.6 10.7 %collective-permute-start.1 = (f32[432,128]{1,0:T(8,128)S(1)}, f32[432,128]{1,0:T(8,128)S(1)}, u32[]{:S(2)}, u32[]{:S(2)}) collective-permute-start(f32[432,128]{1,0:T(8,128)S(1)} %get-tuple-element.18), channel_id=1, source_target_pairs={{2,4},{4,2},{6,8},{8,6},{10,12},{12,10},{3,5},{5,3},{7,9},{9,7},{1... | collective-permute-start | bytes 663560 | tf_op jit(solution)/shard_map/ppermute | solution.py:667
  16.3 6.5 %collective-permute-start.2 = (f32[128,128]{1,0:T(8,128)S(1)}, f32[128,128]{1,0:T(8,128)S(1)}, u32[]{:S(2)}, u32[]{:S(2)}) collective-permute-start(f32[128,128]{1,0:T(8,128)S(1)} %get-tuple-element.19.mine_ref), channel_id=1, source_target_pairs={{0,1},{1,0},{2,3},{3,2},{4,5},{5,4},{6,7},{7,6},{8,9},{9,8},{10,11... | collective-permute-start | bytes 196616 | tf_op jit(solution)/shard_map/ppermute | solution.py:665
  22.8 13.6 %all-to-all-start.1 = ((f32[16,8,128]{2,1,0:T(8,128)}), f32[16,8,128]{2,1,0:T(8,128)S(1)}, u32[]{:S(2)}, u32[]{:S(2)}) async-start(f32[16,8,128]{2,1,0:T(8,128)} %get-tuple-element.23), calls=%async_computation.1 | async-start | bytes 131072 | tf_op jit(solution)/shard_map/all_to_all | solution.py:670

commit v5 on v4

--- a/solution.py
+++ b/solution.py
@@ -126,10 +126,9 @@
     blocks = weights.shape[0]
     tiles = arrived.shape[0]
     vmem = pl.BlockSpec(memory_space=pltpu.VMEM)
-    hbm = pl.BlockSpec(memory_space=pltpu.HBM)
     return pl.pallas_call(
         air_send_kernel,
-        in_specs=[hbm] * 3 + [vmem] * 3,
+        in_specs=[vmem] * 6,
         out_specs=(vmem, vmem),
         out_shape=(
             pltpu.VMEM((tiles, CAP * ROWS, WIN), jnp.float32),
@@ -142,9 +141,9 @@
         cost_estimate=pl.CostEstimate(flops=blocks * 2 * 16 * 128 * 256, bytes_accessed=2000000, transcendentals=0),
         name="air_send",
     )(
-        left(dest),
-        left(source),
-        left(window),
+        held(dest),
+        held(source),
+        held(window),
         held(arrived.reshape(tiles * CAP * ROWS, WIN)),
         some_air,
         held(weights),
@@ -213,6 +212,8 @@
     sea_v,
     low,
     high,
+    low_u,
+    high_u,
     weights,
     top,
     windows,
@@ -234,7 +235,9 @@
     even = gx % 2 == 0
     at_end = (gx == 0) | (gx == last_gx)
     edge = jnp.where(gy == 0, LANES - 1, 0)
-    span = pl.ds(pl.multiple_of(jnp.where(gy == 0, sea_cols - LANES, 0), LANES), LANES)
+    near_half = jnp.where(gy == 0, 1, 0)
+    span = pl.ds(pl.multiple_of(near_half * LANES, LANES), LANES)
+    far = pl.ds(pl.multiple_of((1 - near_half) * LANES, LANES), LANES)
     a, o = air_levels // CHUNKS, sea_levels // CHUNKS
 
     tops = [pltpu.make_async_copy(ocean_ref.at[f, 0], top.at[i], top_sems.at[i]) for i, f in enumerate((0, 2, 3))]
@@ -246,8 +249,10 @@
             (atm_ref.at[:, air_span], air.at[:, air_span]),
             (ocean_ref.at[pl.ds(0, 2), sea_span, :, span], sea.at[:, sea_span]),
             (ocean_ref.at[3, sea_span, :, span], sea_v.at[sea_span]),
-            (ocean_ref.at[pl.ds(0, 3), sea_span, pl.ds(0, SUB)], low.at[:, sea_span]),
-            (ocean_ref.at[pl.ds(0, 3), sea_span, pl.ds(sea_rows - SUB, SUB)], high.at[:, sea_span]),
+            (ocean_ref.at[pl.ds(0, 2), sea_span, pl.ds(0, SUB), far], low.at[:, sea_span]),
+            (ocean_ref.at[pl.ds(0, 2), sea_span, pl.ds(sea_rows - SUB, SUB), far], high.at[:, sea_span]),
+            (ocean_ref.at[2, sea_span, pl.ds(0, SUB)], low_u.at[sea_span]),
+            (ocean_ref.at[2, sea_span, pl.ds(sea_rows - SUB, SUB)], high_u.at[sea_span]),
         ]
         return [pltpu.make_async_copy(src, dst, sems.at[chunk, i]) for i, (src, dst) in enumerate(pairs)]
 
@@ -300,14 +305,16 @@
             total = put(total, sea[0, level], level, sea_lane)
             total = put(total, sea[1, level], sea_levels + level, sea_lane)
             total = put(total, sea_v[level], 2 * sea_levels + level, sea_lane)
-            for f in range(3):
-                for h in range(halves):
-                    tile = pl.ds(h * WIN, WIN)
-                    put_rows(
-                        3 * pitch + (f * halves + h) * sea_levels + level,
-                        low[f, level, pl.ds(0, 1), tile],
-                        high[f, level, pl.ds(SUB - 1, 1), tile],
-                    )
+            at = 3 * pitch + level
+            for f in range(2):
+                near_rows = sea[f, level, pl.ds(0, 1), :], sea[f, level, pl.ds(sea_rows - 1, 1), :]
+                far_rows = low[f, level, pl.ds(0, 1), :], high[f, level, pl.ds(SUB - 1, 1), :]
+                put_rows(at + (f * halves + near_half) * sea_levels, *near_rows)
+                put_rows(at + (f * halves + 1 - near_half) * sea_levels, *far_rows)
+            for h in range(halves):
+                tile = pl.ds(h * WIN, WIN)
+                u_rows = low_u[level, pl.ds(0, 1), tile], high_u[level, pl.ds(SUB - 1, 1), tile]
+                put_rows(at + (2 * halves + h) * sea_levels, *u_rows)
     y_ref[:air_rows] = tracers
     y_ref[air_rows : 2 * air_rows] = v
     y_ref[2 * air_rows :] = total
@@ -336,8 +343,10 @@
             pltpu.VMEM(atm.shape, jnp.float32),
             pltpu.VMEM((2, sea_levels, sea_rows, LANES), jnp.float32),
             pltpu.VMEM((sea_levels, sea_rows, LANES), jnp.float32),
-            pltpu.VMEM((3, sea_levels, SUB, sea_cols), jnp.float32),
-            pltpu.VMEM((3, sea_levels, SUB, sea_cols), jnp.float32),
+            pltpu.VMEM((2, sea_levels, SUB, LANES), jnp.float32),
+            pltpu.VMEM((2, sea_levels, SUB, LANES), jnp.float32),
+            pltpu.VMEM((sea_levels, SUB, sea_cols), jnp.float32),
+            pltpu.VMEM((sea_levels, SUB, sea_cols), jnp.float32),
             pltpu.VMEM(weights.shape, jnp.float32),
             pltpu.VMEM((3, sea_rows, sea_cols), jnp.float32),
             pltpu.VMEM((3, sea_rows * sea_cols // WIN, WIN), jnp.float32),
@@ -346,7 +355,7 @@
             pltpu.SMEM((blocks,), jnp.int32),
             pltpu.SMEM((blocks,), jnp.int32),
             pltpu.SMEM((blocks,), jnp.int32),
-            pltpu.SemaphoreType.DMA((CHUNKS, 5)),
+            pltpu.SemaphoreType.DMA((CHUNKS, 7)),
             pltpu.SemaphoreType.DMA(()),
             pltpu.SemaphoreType.DMA((3,)),
             pltpu.SemaphoreType.DMA((3,)),
@@ -454,13 +463,13 @@
             atm_ref.at[:, levels], air.at[:, levels, pl.ds(PAD, air_rows)], in_sems.at[step, halves]
         )
 
-    def sea_in(step):
-        levels = pl.ds(step * o, o)
+    def sea_in(start, count, sem):
+        levels = pl.ds(start, count)
         for h in range(halves):
             yield pltpu.make_async_copy(
                 ocean_ref.at[:, levels, :, pl.ds(h * LANES, LANES)],
                 sea.at[h, :, levels, pl.ds(PAD, sea_rows)],
-                in_sems.at[step, h],
+                in_sems.at[sem, h],
             )
 
     def air_out(step):
@@ -471,8 +480,11 @@
         levels = pl.ds(step * o, o)
         return pltpu.make_async_copy(sea_new.at[:, levels], sea_ref.at[:, levels], out_sems.at[step, 1])
 
-    for step in range(STEPS):
-        for copy in (*sea_in(step), *(air_in(step) if step > 0 else ())):
+    half = o // 2
+    for copy in (*sea_in(0, half, 0), *sea_in(half, half, STEPS)):
+        copy.start()
+    for step in range(1, STEPS):
+        for copy in (*sea_in(step * o, o, step), *air_in(step)):
             copy.start()
     matrix[...] = shift_matrix()
     air[:, :a, pl.ds(PAD, air_rows), :] = some_air_ref[...]
@@ -535,9 +547,9 @@
         for *place, new in stores:
             air_new[tuple(place)] = new
 
-    def some_sea(step):
-        for j in range(o):
-            level = step * o + j
+    def some_sea(start, count):
+        for j in range(count):
+            level = start + j
             for f in range(3):
                 for h in range(halves):
                     before, after = x_rows(3 * pitch + (f * halves + h) * all_sea + level)
@@ -545,11 +557,11 @@
                     sea[h, f, level, pl.ds(PAD + sea_rows, 1), :] = after
         for i, f in enumerate(SHIFTED):
             for h in range(halves):
-                rows = sea[h, f, pl.ds(step * o, o), pl.ds(PAD, sea_rows), :].reshape(o * sea_rows, LANES)
-                sea_shifted[i, h] = shifted_rows((0.25 * time_step if f == 3 else 1.0) * rows, matrix[...])
+                rows = sea[h, f, pl.ds(start, count), pl.ds(PAD, sea_rows), :].reshape(count * sea_rows, LANES)
+                sea_shifted[i, h, : count * sea_rows] = shifted_rows((0.25 * time_step if f == 3 else 1.0) * rows, matrix[...])
         stores = []
-        for j in range(o):
-            level = step * o + j
+        for j in range(count):
+            level = start + j
             columns = {}
 
             def beyond(f, r, h):
@@ -578,26 +590,25 @@
         air_new[f, 0] = air_new[f, 0] + time_step * flux_ref[f]
     air_out(0).start()
 
+    for start, sem in ((0, 0), (half, STEPS)):
+        for copy in sea_in(start, half, sem):
+            copy.wait()
+        some_sea(start, half)
+    sea_out(0).start()
+    top_ref[...] = sea_new[:, 0]
+
     def some_levels(step, carry):
-        for copy in sea_in(step):
+        for copy in sea_in(step * o, o, step):
             copy.wait()
-        some_sea(step)
+        some_sea(step * o, o)
         sea_out(step).start()
-
-        @pl.when(step == 0)
-        def _():
-            top_ref[...] = sea_new[:, 0]
-
-        @pl.when(step > 0)
-        def _():
-            for copy in air_in(step):
-                copy.wait()
-            some_air(step)
-            air_out(step).start()
-
+        for copy in air_in(step):
+            copy.wait()
+        some_air(step)
+        air_out(step).start()
         return carry
 
-    lax.fori_loop(0, STEPS, some_levels, 0)
+    lax.fori_loop(1, STEPS, some_levels, 0)
     for step in range(STEPS):
         air_out(step).wait()
         sea_out(step).wait()
@@ -629,7 +640,7 @@
             pltpu.VMEM((len(SHIFTED), air_levels // STEPS * air_rows, 2 * LANES), jnp.float32),
             pltpu.VMEM((len(SHIFTED), halves, sea_levels // STEPS * sea_rows, 2 * LANES), jnp.float32),
             pltpu.VMEM((2 * LANES, 2 * LANES), jnp.bfloat16),
-            pltpu.SemaphoreType.DMA((STEPS, halves + 1)),
+            pltpu.SemaphoreType.DMA((STEPS + 1, halves + 1)),
             pltpu.SemaphoreType.DMA((STEPS, 2)),
         ],
         compiler_params=pltpu.CompilerParams(vmem_limit_bytes=VMEM_LIMIT),
@@ -652,7 +663,7 @@
     air_window,
 ):
     width_x, width_y = lax.axis_size("gx"), lax.axis_size("gy")
-    assert width_y == 2 and width_x % 2 == 0
+    assert width_y == 2 and width_x % 2 == 0 and ocean_fields.shape[3] == 2 * LANES
     tiles = width_x * width_y
     exchange = functools.partial(lax.all_to_all, axis_name=("gx", "gy"), split_axis=0, concat_axis=0, tiled=True)
     pairs = [(i, i ^ 1) for i in range(width_x)]

time: 37.6 us -> 37.1 us (0.987)
  Pallas kernels: 18.8 us -> 18.2 us
  transfers between devices with their start and end apart: 5 -> 5, of which waited for: 1 -> 1; matrix products, arithmetic and copies ran while one was open for 0% -> 0% of each run, Pallas kernels for 33% -> 32%
where the time goes in v5:
time: 37.1 us; the launch traced here: 36.8 us
  Pallas kernels  18.2 us (49%)
  starting transfers between devices  13.6 us (37%)
  waiting for transfers between devices  4.23 us (11%)
  between operations  0.78 us (2%)
    pallas_call x1, Pallas kernels, transport(): pl.pallas_call(transport_kernel, in_specs=[hbm, hbm] + [vmem] * 7, out_sp...  9.91 us
    all_to_all x1, starting transfers between devices, body(): on_air = exchange(to_air)  7.4 us
    pallas_call x1, Pallas kernels, first(): pl.pallas_call(first_kernel, in_specs=[hbm] * 6, out_specs=[vmem] * 5, ou...  5.44 us
    all_to_all x1, waiting for transfers between devices, body(): on_air = exchange(to_air)  4.22 us
    all_to_all x1, starting transfers between devices, body(): on_sea = exchange(to_sea)  3.51 us
    ppermute x1, starting transfers between devices, body(): rows = lax.ppermute(rows, 'gx', pairs)  1.93 us
    pallas_call x1, Pallas kernels, air_send(): pl.pallas_call(air_send_kernel, in_specs=[vmem] * 6, out_specs=(vmem, vme...  1.89 us
    pallas_call x1, Pallas kernels, add_sea_forcing(): pl.pallas_call(sea_forcing_kernel, in_specs=[vmem, vmem, vmem, hbm], out_...  1 us
  transfers between devices with their start and end apart: 5, of which 1 were waited for; matrix products, arithmetic and copies ran while one was open for 0% of the time, Pallas kernels for 32%

profile of v5, /device:TPU:0, one launch (start us, length us, event | category | flops | bytes accessed | tf_op | source)
XLA Modules:
  0.0 36.8 jit_solution(8428740111951429432)
XLA Ops:
  0.6 0.0 copy-start
  0.6 0.0 copy-start.2
  0.7 0.0 copy-start.3
  0.7 0.0 copy-start.4
  0.7 0.0 copy-start.1
  0.7 5.4 %first.1 = (f32[16,8,128]{2,1,0:T(8,128)}, f32[432,128]{1,0:T(8,128)S(1)}, f32[432,128]{1,0:T(8,128)S(1)}, f32[128,128]{1,0:T(8,128)S(1)}, f32[4,12,32,128]{3,2,1,0:T(8,128)S(1)}) custom-call(s32[24]{0:T(128)} %bitcast.7, s32[24]{0:T(128)} %source_hbm.2, s32[24]{0:T(128)} %window_hbm.2, f32[4,60,32,128]{3,2,1,0:T(8,128)} %atm_ref.3, ...), custom_call_target="tpu_custom_call" | custom-call | flops 30000000 | bytes 12000000 | tf_op jit(solution)/shard_map/first/pallas_call | solution.py:331
  6.1 7.4 %all-to-all-start = ((f32[16,8,128]{2,1,0:T(8,128)}), f32[16,8,128]{2,1,0:T(8,128)S(1)}, u32[]{:S(2)}, u32[]{:S(2)}) async-start(f32[16,8,128]{2,1,0:T(8,128)} %get-tuple-element.15), calls=%async_computation | async-start | bytes 131072 | tf_op jit(solution)/shard_map/all_to_all | solution.py:675
  13.5 1.9 %collective-permute-start = (f32[432,128]{1,0:T(8,128)S(1)}, f32[432,128]{1,0:T(8,128)S(1)}, u32[]{:S(2)}, u32[]{:S(2)}) collective-permute-start(f32[432,128]{1,0:T(8,128)S(1)} %get-tuple-element.17), channel_id=1, source_target_pairs={{0,2},{2,0},{4,6},{6,4},{8,10},{10,8},{12,14},{14,12},{1,3},{3,1},... | collective-permute-start | bytes 663560 | tf_op jit(solution)/shard_map/ppermute | solution.py:677
  15.5 0.7 %collective-permute-start.1 = (f32[432,128]{1,0:T(8,128)S(1)}, f32[432,128]{1,0:T(8,128)S(1)}, u32[]{:S(2)}, u32[]{:S(2)}) collective-permute-start(f32[432,128]{1,0:T(8,128)S(1)} %get-tuple-element.18), channel_id=1, source_target_pairs={{2,4},{4,2},{6,8},{8,6},{10,12},{12,10},{3,5},{5,3},{7,9},{9,7},{1... | collective-permute-start | bytes 663560 | tf_op jit(solution)/shard_map/ppermute | solution.py:678
  16.1 0.1 collective-permute-start.2
  16.2 4.2 %all-to-all-done = f32[16,8,128]{2,1,0:T(8,128)S(1)} async-done(((f32[16,8,128]{2,1,0:T(8,128)}), f32[16,8,128]{2,1,0:T(8,128)S(1)}, u32[]{:S(2)}, u32[]{:S(2)}) %all-to-all-start) | async-done | bytes 65568 | tf_op jit(solution)/shard_map/all_to_all | solution.py:675
  20.4 0.0 copy-done
  20.4 0.0 copy-done.2
  20.4 0.0 copy-done.3
  20.4 0.0 copy-done.4
  20.5 1.9 %air_send.1 = (f32[16,8,128]{2,1,0:T(8,128)}, f32[2,32,128]{2,1,0:T(8,128)S(1)}) custom-call(s32[24]{0:T(128)S(1)} %bitcast.6, s32[24]{0:T(128)S(1)} %copy-done.3, s32[24]{0:T(128)S(1)} %copy-done.4, f32[128,128]{1,0:T(8,128)S(1)} %bitcast.5, f32[4,12,32,128]{3,2,1,0:T(8,128)S(1)} %get-tuple-element.14.some_air_ref, f32[24,128,128]{2,1,0:T(8,128)S(1)} %copy-done), custom_call_target="tpu_custom_call" | custom-call | flops 25165824 | bytes 2000000 | tf_op jit(solution)/shard_map/air_send/pallas_call | solution.py:129
  22.4 0.0 collective-permute-done.2.y_ref
  22.4 3.5 %all-to-all-start.1 = ((f32[16,8,128]{2,1,0:T(8,128)}), f32[16,8,128]{2,1,0:T(8,128)S(1)}, u32[]{:S(2)}, u32[]{:S(2)}) async-start(f32[16,8,128]{2,1,0:T(8,128)} %get-tuple-element.23), calls=%async_computation.1 | async-start | bytes 131072 | tf_op jit(solution)/shard_map/all_to_all | solution.py:681
  25.9 0.0 collective-permute-done.first_ref
  25.9 0.0 collective-permute-done.1.second_ref
  25.9 0.0 copy-done.1
  25.9 9.9 %transport.1 = (f32[2,60,32,128]{3,2,1,0:T(8,128)}, f32[2,40,64,256]{3,2,1,0:T(8,128)}, f32[2,64,256]{2,1,0:T(8,128)S(1)}) custom-call(f32[4,60,32,128]{3,2,1,0:T(8,128)} %atm_ref.3, f32[4,40,64,256]{3,2,1,0:T(8,128)} %ocean_ref.3, f32[4,12,32,128]{3,2,1,0:T(8,128)S(1)} %get-tuple-element.14.some_air_ref, s32[64,256]{1,0:T(8,128)S(1)} %copy-done.1, ...), custom_call_target="tpu_custom_call" | custom-call | flops 60000000 | bytes 22000000 | tf_op jit(solution)/shard_map/transport/pallas_call | solution.py:624
  35.8 0.0 all-to-all-done.1
  35.8 1.0 %sea_forcing.1 = f32[2,40,64,256]{3,2,1,0:T(8,128)} custom-call(f32[128,128]{1,0:T(8,128)S(1)} %bitcast.4, s32[64,256]{1,0:T(8,128)S(1)} %copy-done.1, f32[2,64,256]{2,1,0:T(8,128)S(1)} %get-tuple-element.24.top_ref, f32[2,40,64,256]{3,2,1,0:T(8,128)} %get-tuple-element.25.before_ref), custom_call_target="tpu_custom_call", output_to_operand_aliasing={{}: (3, {})} | custom-call | flops 4000000 | bytes 600000 | tf_op jit(solution)/shard_map/sea_forcing/pallas_call | solution.py:174
Async XLA Ops:
  0.6 19.8 %copy-start = (f32[24,128,128]{2,1,0:T(8,128)S(1)}, f32[24,128,128]{2,1,0:T(8,128)}, u32[]{:S(2)}) copy-start(f32[24,128,128]{2,1,0:T(8,128)} %weights_ref.3) | copy-start | bytes 4718596
  0.6 19.8 %copy-start.2 = (s32[24,1]{0,1:T(1,128)S(1)}, s32[24,1]{0,1:T(1,128)}, u32[]{:S(2)}) copy-start(s32[24,1]{0,1:T(1,128)} %param.19) | copy-start | bytes 292
  0.7 19.8 %copy-start.3 = (s32[24]{0:T(128)S(1)}, s32[24]{0:T(128)}, u32[]{:S(2)}) copy-start(s32[24]{0:T(128)} %source_hbm.3) | copy-start | bytes 292
  0.7 19.8 %copy-start.4 = (s32[24]{0:T(128)S(1)}, s32[24]{0:T(128)}, u32[]{:S(2)}) copy-start(s32[24]{0:T(128)} %window_hbm.3) | copy-start | bytes 292
  0.7 25.2 %copy-start.1 = (s32[64,256]{1,0:T(8,128)S(1)}, s32[64,256]{1,0:T(8,128)}, u32[]{:S(2)}) copy-start(s32[64,256]{1,0:T(8,128)} %land_ref.3) | copy-start | bytes 196612
  6.1 14.3 %all-to-all-start = ((f32[16,8,128]{2,1,0:T(8,128)}), f32[16,8,128]{2,1,0:T(8,128)S(1)}, u32[]{:S(2)}, u32[]{:S(2)}) async-start(f32[16,8,128]{2,1,0:T(8,128)} %get-tuple-element.15), calls=%async_computation | async-start | bytes 131072 | tf_op jit(solution)/shard_map/all_to_all | solution.py:675
  13.5 12.3 %collective-permute-start = (f32[432,128]{1,0:T(8,128)S(1)}, f32[432,128]{1,0:T(8,128)S(1)}, u32[]{:S(2)}, u32[]{:S(2)}) collective-permute-start(f32[432,128]{1,0:T(8,128)S(1)} %get-tuple-element.17), channel_id=1, source_target_pairs={{0,2},{2,0},{4,6},{6,4},{8,10},{10,8},{12,14},{14,12},{1,3},{3,1},... | collective-permute-start | bytes 663560 | tf_op jit(solution)/shard_map/ppermute | solution.py:677
  15.5 10.4 %collective-permute-start.1 = (f32[432,128]{1,0:T(8,128)S(1)}, f32[432,128]{1,0:T(8,128)S(1)}, u32[]{:S(2)}, u32[]{:S(2)}) collective-permute-start(f32[432,128]{1,0:T(8,128)S(1)} %get-tuple-element.18), channel_id=1, source_target_pairs={{2,4},{4,2},{6,8},{8,6},{10,12},{12,10},{3,5},{5,3},{7,9},{9,7},{1... | collective-permute-start | bytes 663560 | tf_op jit(solution)/shard_map/ppermute | solution.py:678
  16.1 6.2 %collective-permute-start.2 = (f32[128,128]{1,0:T(8,128)S(1)}, f32[128,128]{1,0:T(8,128)S(1)}, u32[]{:S(2)}, u32[]{:S(2)}) collective-permute-start(f32[128,128]{1,0:T(8,128)S(1)} %get-tuple-element.19.mine_ref), channel_id=1, source_target_pairs={{0,1},{1,0},{2,3},{3,2},{4,5},{5,4},{6,7},{7,6},{8,9},{9,8},{10,11... | collective-permute-start | bytes 196616 | tf_op jit(solution)/shard_map/ppermute | solution.py:676
  22.4 13.5 %all-to-all-start.1 = ((f32[16,8,128]{2,1,0:T(8,128)}), f32[16,8,128]{2,1,0:T(8,128)S(1)}, u32[]{:S(2)}, u32[]{:S(2)}) async-start(f32[16,8,128]{2,1,0:T(8,128)} %get-tuple-element.23), calls=%async_computation.1 | async-start | bytes 131072 | tf_op jit(solution)/shard_map/all_to_all | solution.py:681
